TPU v7x, 256 devices: a whole 4x4x8 slice. The times are simulated.
256 devices in a mesh: tm: 8 (over y, x_hi), dp: 32 (over z, x_lo, core).
Axes of the slice: x: 4 (x_hi: 2, x_lo: 2; x = x_hi * 2 + x_lo), y: 4, z: 8, core: 2. Of those that a mesh axis runs over, the one named last changes fastest.
Arguments:
- features: bfloat16 [32, 32, 2, 8, 256], P('dp', 'tm'), may hold values from -6 to 6
- upstream: bfloat16 [32, 32, 4, 16, 128], P('dp', 'tm'), may hold values from -6 to 6
- weight_one: bfloat16 [3, 3, 3, 256, 128], replicated, may hold values from -0.078125 to 0.078125
- weight_two: bfloat16 [3, 3, 3, 128, 128], replicated, may hold values from -0.109375 to 0.109375
Outputs:
- feature_grad: bfloat16 [32, 32, 2, 8, 256], P('dp', 'tm')
- grad_one: float32 [3, 3, 3, 256, 128], P(None, None, None, 'dp')
- grad_two: float32 [3, 3, 3, 128, 128], P(None, None, None, 'dp')
All inputs are finite; a program needn't handle non-finite values.
Results may differ from a plain program's by a relative error of at most 0.0049.
Values may be sent and summed in bfloat16 or wider, within the bound.
A program may use at most 64 MiB of HBM per device.

v0:
```python
import math

import jax
import jax.numpy as jnp
from jax import lax
from jax.sharding import PartitionSpec as P


def passed_along(value, axis, by):
    size = lax.axis_size(axis)
    pairs = [(i, i + by) for i in range(size) if 0 <= i + by < size]
    return lax.ppermute(value, axis, pairs)


def upsample(values):
    return jnp.repeat(jnp.repeat(values, 2, axis=2), 2, axis=3)


def forward_conv(padded, kernel):
    return lax.conv_general_dilated(
        padded,
        kernel,
        (1, 1, 1),
        "VALID",
        dimension_numbers=("NDHWC", "DHWIO", "NDHWC"),
        preferred_element_type=jnp.float32,
    )


def kernel_grad(padded, cotangent):
    return lax.conv_general_dilated(
        padded,
        cotangent,
        (1, 1, 1),
        "VALID",
        dimension_numbers=("CDHWN", "IDHWO", "DHWNC"),
        preferred_element_type=jnp.float32,
    )


def data_grad(cotangent, kernel):
    return lax.conv_general_dilated(
        cotangent,
        kernel[::-1, ::-1, ::-1],
        (1, 1, 1),
        [(2, 2), (2, 2), (2, 2)],
        dimension_numbers=("NDHWC", "DHWOI", "NDHWC"),
        preferred_element_type=jnp.float32,
    )


def pad_space(values):
    return jnp.pad(values, ((0, 0), (0, 0), (1, 1), (1, 1), (0, 0)))


def pad_front(values, frames_dev):
    return jnp.pad(values, ((0, 0), (frames_dev - 2, 0), (0, 0), (0, 0), (0, 0)))


def silu_slope(pre):
    sigma = jax.nn.sigmoid(pre)
    return sigma * (1.0 + pre * (1.0 - sigma))


def pool_pairs(values):
    shape = values.shape
    return values.reshape(shape[0], shape[1], shape[2] // 2, 2, shape[3] // 2, 2, shape[4]).sum(
        axis=(3, 5)
    )


def on_device(features, upstream, weight_one, weight_two):
    frames_dev = features.shape[1]
    earlier = passed_along(features, "tm", 1)
    padded_all = pad_space(upsample(jnp.concatenate([earlier, features], axis=1)))
    pre_all = forward_conv(padded_all, weight_one)
    padded = padded_all[:, 2:]
    pre = pre_all[:, 2:]
    hidden_all = jax.nn.silu(pre_all).astype(jnp.bfloat16)
    grad_second = kernel_grad(pad_space(hidden_all), upstream)
    back_all = data_grad(upstream, weight_two)[:, :, 1:-1, 1:-1]
    later_back = passed_along(back_all[:, :2], "tm", -1)
    back = back_all[:, 2:] + pad_front(later_back, frames_dev)
    dpre = (back * silu_slope(pre)).astype(jnp.bfloat16)
    grad_first = kernel_grad(padded, dpre)
    pooled = pool_pairs(data_grad(dpre, weight_one)[:, :, 1:-1, 1:-1])
    later_pooled = passed_along(pooled[:, :2], "tm", -1)
    feature_grad = (pooled[:, 2:] + pad_front(later_pooled, frames_dev)).astype(jnp.bfloat16)
    totals = lax.psum((grad_first, grad_second), "tm")
    shares = (
        lax.psum_scatter(totals[0], "dp", scatter_dimension=3, tiled=True),
        lax.psum_scatter(totals[1], "dp", scatter_dimension=3, tiled=True),
    )
    count = (
        features.shape[0]
        * lax.axis_size("dp")
        * frames_dev
        * lax.axis_size("tm")
        * upstream.shape[2]
        * upstream.shape[3]
    )
    factor = 1.0 / math.sqrt(count)
    return (feature_grad, shares[0] * factor, shares[1] * factor)


def solution(mesh):
    in_specs = (P("dp", "tm", None, None, None), P("dp", "tm", None, None, None), P(), P())
    out_specs = (
        P("dp", "tm", None, None, None),
        P(None, None, None, "dp", None),
        P(None, None, None, "dp", None),
    )
    return jax.shard_map(
        on_device, mesh=mesh, in_specs=in_specs, out_specs=out_specs, check_vma=False
    )
```

profile of v0, /device:TPU:2, one launch (start us, length us, event | category | flops | bytes accessed | tf_op | source)
XLA Modules:
  0.0 476.6 jit_solution(17566672928204509618)
XLA Ops:
  7.2 0.0 copy-start
  7.2 0.0 all-reduce.8.cloned.1.call-start
  7.2 4.2 collective-permute-start.1
  11.4 0.9 copy.49
  12.3 0.1 fusion.51
  12.4 0.0 copy-start.1
  12.4 2.4 convolution_select_fusion.2
  14.8 0.0 copy-start.3
  14.8 1.3 collective-permute-start
  16.2 0.1 copy.30
  16.2 0.0 collective-permute-done.1
  16.2 0.0 copy-done.1
  16.4 0.1 copy.34
  16.5 0.1 slice.48
  16.5 0.0 copy-done
  16.5 0.0 copy-done.3
  16.6 2.2 fusion.31
  18.9 2.4 convolution_bitcast_fusion
  21.3 0.1 add_multiply_fusion
  21.4 0.1 copy.35
  21.4 0.0 all-reduce.8.cloned.1.call-update
  21.5 0.0 reduce-scatter.3.cloned.1.call-start
  21.5 1.0 collective-permute-done
  22.6 5.6 %fusion.7 = f32[3,3,3,256,128]{4,3,2,1,0:T(8,128)} fusion(bf16[1,8,4,16,256]{4,1,3,2,0:T(8,128)(2,1)S(1)} %bitcast.62, bf16[1,4,4,16,128]{4,2,3,1,0:T(4,128)(2,1)S(1)} %fusion.33), kind=kOutput, calls=%fused_computation.11 | convolution fusion | flops 361758720 | bytes 3866624 | tf_op jit(solution)/shard_map/conv_general_dilated | solution.py:31
  28.2 0.0 reduce-scatter.3.cloned.1.call-update
  28.2 0.0 all-reduce.6.cloned.1.call-start
  28.4 1.3 convolution_select_fusion
  29.7 0.0 copy-start.2
  29.7 0.2 copy.40
  30.0 0.3 reshape.19
  30.3 0.3 reduce_sum.11
  30.7 1.3 collective-permute-start.2
  32.0 0.0 copy-done.2
  32.0 0.6 dynamic-slice
  33.2 4.8 collective-permute-done.2
  38.0 0.6 copy.46
  38.6 214.1 %all-reduce.8.cloned.1.call-done = f32[3,3,3,128,128]{4,3,2,1,0:T(8,128)} async-done(((f32[3,3,3,128,128]{4,3,2,1,0:T(8,128)}), f32[3,3,3,128,128]{4,3,2,1,0:T(8,128)}) %all-reduce.8.cloned.1.call-update) | async-done | bytes 1769488
  252.7 0.9 constant_dynamic-slice_fusion
  253.6 41.8 %psum.17 = f32[3,3,3,4,128]{4,3,2,1,0:T(4,128)S(1)} all-reduce(f32[3,3,3,4,128]{4,3,2,1,0:T(4,128)S(1)} %constant_dynamic-slice_fusion), channel_id=1, replica_groups=mesh['tm'=8,'dp'=32] {'tm'}, use_global_device_ids=true, to_apply=%region_3.4 | all-reduce | flops 13824 | bytes 110592 | tf_op jit(solution)/shard_map/psum | solution.py:89
  295.4 81.7 %reduce-scatter.3.cloned.1.call-done = f32[3,3,3,8,128]{4,3,2,1,0:T(8,128)} async-done(((f32[3,3,3,256,128]{4,3,2,1,0:T(8,128)}), f32[3,3,3,8,128]{4,3,2,1,0:T(8,128)}) %reduce-scatter.3.cloned.1.call-update) | async-done | bytes 110608 | tf_op jit(solution)/shard_map/reduce_scatter | solution.py:91
  377.1 0.0 all-reduce.6.cloned.1.call-update
  377.1 0.6 broadcast_multiply_fusion.1
  377.7 90.8 %all-reduce.6.cloned.1.call-done = f32[3,3,3,8,128]{4,3,2,1,0:T(8,128)} async-done(((f32[3,3,3,8,128]{4,3,2,1,0:T(8,128)}), f32[3,3,3,8,128]{4,3,2,1,0:T(8,128)}) %all-reduce.6.cloned.1.call-update) | async-done | bytes 110608 | tf_op jit(solution)/shard_map/psum | solution.py:89
  468.5 1.5 broadcast_multiply_fusion
  (23 shorter events, 0.5 us)
Async XLA Ops:
  7.2 9.4 %copy-start = (bf16[3,3,3,256,128]{4,3,2,1,0:T(8,128)(2,1)S(1)}, bf16[3,3,3,256,128]{4,3,2,1,0:T(8,128)(2,1)}, u32[]{:S(2)}) copy-start(bf16[3,3,3,256,128]{4,3,2,1,0:T(8,128)(2,1)} %param.6) | copy-start | bytes 5308420
  7.2 245.5 %all-reduce.8.cloned.1.call-start = ((), (), s32[]{:S(2)}) async-start(), calls=%async_computation.3 | async-start | bytes 3538944
  7.2 9.0 %collective-permute-start.1 = (bf16[1,4,2,8,256]{4,3,2,1,0:T(8,128)(2,1)}, bf16[1,4,2,8,256]{4,3,2,1,0:T(8,128)(2,1)S(1)}, u32[]{:S(2)}, u32[]{:S(2)}) collective-permute-start(bf16[1,4,2,8,256]{4,3,2,1,0:T(8,128)(2,1)} %param.4), channel_id=1, source_target_pairs={{0,32},{32,64},{64,96},{96,128},{128,160},{160,192},{192,224},{1,3... | collective-permute-start | bytes 98312 | tf_op jit(solution)/shard_map/ppermute | solution.py:12
  12.4 3.9 copy-start.1
  14.8 1.7 copy-start.3
  14.8 7.7 %collective-permute-start = (f32[1,2,4,16,128]{4,2,3,1,0:T(4,128)S(1)}, f32[1,2,4,16,128]{4,2,3,1,0:T(4,128)S(1)}, u32[]{:S(2)}, u32[]{:S(2)}) collective-permute-start(f32[1,2,4,16,128]{4,2,3,1,0:T(4,128)S(1)} %slice_bitcast_fusion.2), channel_id=1, source_target_pairs={{32,0},{64,32},{96,64},{128,96},{160,128},{192,160},{224,192},{33,... | collective-permute-start | bytes 196616 | tf_op jit(solution)/shard_map/ppermute | solution.py:12
  21.5 355.6 %reduce-scatter.3.cloned.1.call-start = ((), (), s32[]{:S(2)}) async-start(), calls=%async_computation.1 | async-start | bytes 3649536 | tf_op jit(solution)/shard_map/reduce_scatter | solution.py:91
  28.2 440.3 %all-reduce.6.cloned.1.call-start = ((), (), s32[]{:S(2)}) async-start(), calls=%async_computation.2 | async-start | bytes 221184 | tf_op jit(solution)/shard_map/psum | solution.py:89
  29.7 2.3 copy-start.2
  30.7 7.3 %collective-permute-start.2 = (f32[1,2,2,8,256]{4,2,3,1,0:T(2,128)S(1)}, f32[1,2,2,8,256]{4,2,3,1,0:T(2,128)S(1)}, u32[]{:S(2)}, u32[]{:S(2)}) collective-permute-start(f32[1,2,2,8,256]{4,2,3,1,0:T(2,128)S(1)} %slice.54), channel_id=1, source_target_pairs={{32,0},{64,32},{96,64},{128,96},{160,128},{192,160},{224,192},{33,... | collective-permute-start | bytes 98312 | tf_op jit(solution)/shard_map/ppermute | solution.py:12
Sparse Core Ops, SparseCore 0:
  21.6 231.0 all-reduce.7
  255.4 121.6 reduce-scatter.2
  379.7 88.7 all-reduce.5
where the time goes:
time: 477 us
  waiting for transfers between devices  392 us (82%)
  blocking collectives  41.8 us (9%)
  between operations  14.8 us (3%)
  matrix products  13.9 us (3%)
  starting transfers between devices  6.87 us (1%)
    unnamed x4, waiting for transfers between devices  214 us
    psum x1, waiting for transfers between devices, on_device(): totals = lax.psum((grad_first, grad_second), 'tm')  90.8 us
    reduce_scatter x1, waiting for transfers between devices, on_device(): lax.psum_scatter(totals[0], 'dp', scatter_dimension=3, tiled=True)  81.7 us
    psum x1, blocking collectives, on_device(): totals = lax.psum((grad_first, grad_second), 'tm')  41.8 us
  transfers between devices with their start and end apart: 6, of which 5 were waited for; matrix products, arithmetic and copies ran while one was open for 4% of the time, Pallas kernels for 0%

commit v1 on v0

v1 whole, which is shorter than its diff:
```python
import jax
import jax.numpy as jnp
import numpy as np
from jax import lax
from jax.experimental import pallas as pl
from jax.experimental.pallas import tpu as pltpu
from jax.sharding import PartitionSpec as P

MESH = pl.DeviceIdType.MESH
F32, BF16 = jnp.float32, jnp.bfloat16

NZ, NX, NY, NTM = 8, 4, 4, 8
TILES = 24
HALF = 12


def tables():
    select = np.zeros((256, 576), np.float32)
    for f in range(4):
        for r in range(4):
            for s in range(16):
                for b in range(3):
                    for e in range(3):
                        rr, ss = r + b - 1, s + e - 1
                        if 0 <= rr < 4 and 0 <= ss < 16:
                            select[f * 64 + r * 16 + s, (b * 3 + e) * 64 + f * 16 + rr // 2 * 8 + ss // 2] = 1
    order_one = np.zeros((256, 256), np.float32)
    order_two = np.zeros((512, 384), np.float32)
    for core in range(2):
        for x_lo in range(2):
            for z in range(8):
                d = (core * 2 + x_lo) * 8 + z
                dp = z * 4 + x_lo * 2 + core
                for k in range(8):
                    order_one[d * 8 + k, dp * 8 + k] = 1
                for a in range(3):
                    for k in range(4):
                        order_two[d * 16 + a * 4 + k, a * 128 + dp * 4 + k] = 1
    return [jnp.asarray(m, BF16) for m in (select, select.T, order_one, order_two)]


def dot(a, b):
    return jnp.dot(a, b, preferred_element_type=F32)


def dot_nt(a, b):
    return lax.dot_general(a, b, (((1,), (1,)), ((), ())), preferred_element_type=F32)


def slots(z, t):
    if z < 4:
        return (0, 2 * z + t) if t < 2 else (1, z)
    return (0, 4 + z) if t == 0 else (1, 4 + 2 * (z - 4) + t - 1)


def kernel(
    f_ref, u_ref, w1_ref, w2_ref, up_ref, pool_ref, ord1_ref, ord2_ref,
    fg_ref, g1_ref, g2_ref,
    fh, uh, ystk, u9, hid, slope, dpre, p9,
    ra, rb, ra0, rb0, ra1, rb1, sa, sb, ra2, rb2, zb, rz, share, gath,
    s_halo, r_halo, s_a0, r_a0, s_b0, r_b0, s_a1, r_a1, s_b1, r_b1, s_a2, r_a2, s_b2, r_b2, s_z, r_z, s_g, r_g,
):
    tm, dp = lax.axis_index("tm"), lax.axis_index("dp")
    y, x_hi = tm // 2, tm % 2
    z, x_lo, core = dp // 4, (dp // 2) % 2, dp % 2
    x = x_lo * 2 + x_hi

    def at(xx=x, yy=y, zz=z, cc=core):
        return {"tm": yy * 2 + xx % 2, "dp": zz * 4 + (xx // 2) * 2 + cc}

    def at_tm(t):
        return {"tm": t, "dp": dp}

    barrier = pltpu.get_barrier_semaphore()
    peers = [at_tm((tm + k) % NTM) for k in range(1, NTM)]
    peers += [at(zz=(z + k) % NZ) for k in range(1, NZ)]
    peers += [at(cc=1 - core)]
    other = (1 - x_lo) * 2
    peers += [at(xx=other), at(xx=other + 1)]
    for peer in peers:
        pl.semaphore_signal(barrier, inc=1, device_id=peer, device_id_type=MESH)
    pl.semaphore_wait(barrier, len(peers))

    def send(src, dst, ssem, rsem, to):
        copy = pltpu.make_async_remote_copy(
            src_ref=src, dst_ref=dst, send_sem=ssem, recv_sem=rsem, device_id=to, device_id_type=MESH
        )
        copy.start()
        return copy

    nxt, prv = at_tm((tm + 1) % NTM), at_tm((tm + NTM - 1) % NTM)
    halo = [
        send(f_ref, fh.at[pl.ds(0, 64)], s_halo.at[0], r_halo.at[0], nxt),
        send(f_ref.at[pl.ds(0, 32)], fh.at[pl.ds(128, 32)], s_halo.at[1], r_halo.at[1], prv),
        send(u_ref, uh.at[pl.ds(0, 256)], s_halo.at[2], r_halo.at[2], prv),
    ]
    fh[64:128, :] = f_ref[...]
    column = lax.broadcasted_iota(jnp.int32, (256, 128), 0) % 16

    def shifted(block, first):
        wide = block.astype(F32)
        back_one = jnp.where(column == 15, 0.0, pltpu.roll(wide, 255, 0)).astype(BF16)
        on_one = jnp.where(column == 0, 0.0, pltpu.roll(wide, 1, 0)).astype(BF16)
        zero = jnp.zeros((4, 16, 128), BF16)
        for e, v in enumerate((back_one, block, on_one)):
            v = v.reshape(4, 64, 128)
            for b in range(3):
                tap = slice((b * 3 + e) * 128, (b * 3 + e + 1) * 128)
                if b == 0:
                    rows = jnp.concatenate([v[:, 16:], zero], axis=1)
                elif b == 1:
                    rows = v
                else:
                    rows = jnp.concatenate([zero, v[:, :48]], axis=1)
                u9[first : first + 256, tap] = rows.reshape(256, 128)

    shifted(u_ref[...], 0)

    halo[0].wait()
    halo[1].wait()

    @pl.when(tm == 0)
    def _():
        fh[0:64, :] = jnp.zeros((64, 256), BF16)

    @pl.when(tm == NTM - 1)
    def _():
        fh[128:160, :] = jnp.zeros((32, 256), BF16)

    cat = jnp.concatenate([fh[0:128, :], fh[16:144, :], fh[32:160, :]], axis=1)
    for be in range(9):
        prod = dot(cat, w1_ref[:, be].reshape(768, 128))
        high = prod.astype(BF16)
        low = (prod - high.astype(F32)).astype(BF16)
        for blk in range(2):
            ystk[blk, 0, be * 64 : be * 64 + 64, :] = high[blk * 64 : blk * 64 + 64]
            ystk[blk, 1, be * 64 : be * 64 + 64, :] = low[blk * 64 : blk * 64 + 64]
    for blk in range(2):
        pre = dot(up_ref[...], ystk[blk, 0]) + dot(up_ref[...], ystk[blk, 1])
        sigma = 1.0 / (1.0 + jnp.exp(-pre))
        hid[blk * 256 : blk * 256 + 256, :] = (pre * sigma).astype(BF16)
        slope[blk * 256 : blk * 256 + 256, :] = sigma * (1.0 + pre * (1.0 - sigma))

    halo[2].wait()

    @pl.when(tm == NTM - 1)
    def _():
        uh[...] = jnp.zeros((256, 128), BF16)

    shifted(uh[...], 256)
    back = jnp.zeros((384, 128), F32)
    for a in range(3):
        kern = jnp.concatenate([w2_ref[a, be] for be in range(9)], axis=1)
        back += dot_nt(u9[(2 - a) * 64 : (2 - a) * 64 + 384, :], kern)
    dpre[0:384, :] = (back * slope[128:512, :]).astype(BF16)
    dpre[384:512, :] = jnp.zeros((128, 128), BF16)
    for blk in range(2):
        pooled = dot(pool_ref[...], dpre[blk * 256 : blk * 256 + 256, :]).astype(BF16)
        for be in range(9):
            p9[blk * 64 : blk * 64 + 64, be * 128 : be * 128 + 128] = pooled[be * 64 : be * 64 + 64]

    def put(tile, value):
        j, t = tile // 3, tile % 3
        yy, hh = j // 2, j % 2
        for c in range(2):
            for lo in range(2):
                for zz in range(8):
                    route, slot = slots(zz, t)
                    v = value[(c * 2 + lo) * 8 + zz]
                    if route == 0:
                        ra[c, lo * 2 + hh, yy, slot] = v
                    else:
                        rb[c, yy, lo * 2 + hh, slot] = v

    turned = dot_nt(ord2_ref[...], jnp.concatenate([hid[a * 64 : a * 64 + 256, :] for a in range(3)], axis=1)).astype(BF16)
    for be in range(9):
        two = dot(turned, u9[0:256, be * 128 : be * 128 + 128])
        put(14 + be, two.astype(BF16).reshape(32, 16, 128))
    units = []
    for a in range(3):
        feats = dot_nt(ord1_ref[...], fh[(2 + a) * 16 : (2 + a) * 16 + 64, :]).astype(BF16)
        for be in range(9):
            units.append(dot(feats, p9[0:64, be * 128 : be * 128 + 128]).reshape(32, 8, 128))
            if len(units) == 2:
                put((a * 9 + be) // 2, jnp.concatenate(units, axis=1).astype(BF16))
                units = []
    units.append(jnp.zeros((32, 8, 128), F32))
    put(13, jnp.concatenate(units, axis=1).astype(BF16))
    put(23, jnp.zeros((32, 16, 128), BF16))

    mate = at(cc=1 - core)
    first = []
    for k in (1, 2, 3, 0):
        xd, yd = (x + k) % NX, (y + k) % NY
        first.append((
            k,
            send(ra.at[1 - core, xd], ra0.at[xd], s_a0.at[k], r_a0.at[k], mate),
            send(rb.at[1 - core, yd], rb0.at[yd], s_b0.at[k], r_b0.at[k], mate),
        ))

    result = jnp.zeros((64, 256), F32)
    for a in range(3):
        kern = jnp.concatenate([w1_ref[a, be] for be in range(9)], axis=1)
        result += dot_nt(p9[(2 - a) * 16 : (2 - a) * 16 + 64, :], kern)
    fg_ref[...] = result.astype(BF16)

    second_a, second_b = [], []
    for k, copy_a, copy_b in first:
        xd, yd = (x + k) % NX, (y + k) % NY
        copy_a.wait_recv()
        ra[core, xd] = (ra[core, xd].astype(F32) + ra0[xd].astype(F32)).astype(BF16)
        if k:
            second_a.append(send(ra.at[core, xd], ra1.at[k - 1], s_a1.at[k - 1], r_a1.at[k - 1], at(xx=xd)))
        copy_b.wait_recv()
        rb[core, yd] = (rb[core, yd].astype(F32) + rb0[yd].astype(F32)).astype(BF16)
        if k:
            second_b.append(send(rb.at[core, yd], rb1.at[k - 1], s_b1.at[k - 1], r_b1.at[k - 1], at(yy=yd)))

    for copy in second_a + second_b:
        copy.wait_recv()
    sums_a = ra[core, x].astype(F32)
    sums_b = rb[core, y].astype(F32)
    for k in range(3):
        sums_a += ra1[k].astype(F32)
        sums_b += rb1[k].astype(F32)
    sa[...] = sums_a.astype(BF16)
    sb[...] = sums_b.astype(BF16)
    third = []
    for k in range(1, 4):
        xd, yd = (x + k) % NX, (y + k) % NY
        third.append(send(sa.at[yd], ra2.at[k - 1], s_a2.at[k - 1], r_a2.at[k - 1], at(yy=yd)))
        third.append(send(sb.at[xd], rb2.at[k - 1], s_b2.at[k - 1], r_b2.at[k - 1], at(xx=xd)))
    for copy in third:
        copy.wait_recv()
    ends = [sa[y].astype(F32), sb[x].astype(F32)]
    for k in range(3):
        ends[0] += ra2[k].astype(F32)
        ends[1] += rb2[k].astype(F32)
    ends = [v.astype(BF16) for v in ends]
    for zz in range(8):
        for t in range(3):
            route, slot = slots(zz, t)
            zb[zz, t * 16 : t * 16 + 16, :] = ends[route][slot]
    fourth = []
    for k in range(1, 8):
        zd = (z + k) % NZ
        fourth.append(send(zb.at[zd], rz.at[k - 1], s_z.at[k - 1], r_z.at[k - 1], at(zz=zd)))
    for copy in fourth:
        copy.wait_recv()
    total = zb[z].astype(F32)
    for k in range(7):
        total += rz[k].astype(F32)
    total *= 1.0 / 256.0
    share[...] = total
    gath[tm] = total
    fifth = []
    for k in range(1, 8):
        fifth.append(send(share, gath.at[tm], s_g.at[k - 1], r_g.at[k - 1], at_tm((tm + k) % NTM)))
    for copy in fifth:
        copy.wait_recv()
    for tile in range(23):
        rows = gath[tile // 3, tile % 3 * 16 : tile % 3 * 16 + 16, :]
        if tile < 14:
            g1_ref[2 * tile] = rows[0:8]
            if tile < 13:
                g1_ref[2 * tile + 1] = rows[8:16]
        else:
            for a in range(3):
                g2_ref[a * 9 + tile - 14] = rows[a * 4 : a * 4 + 4]

    for k, copy_a, copy_b in first:
        copy_a.wait_send()
        copy_b.wait_send()
    for copy in second_a + second_b + third + fourth + fifth:
        copy.wait_send()


def on_device(features, upstream, weight_one, weight_two):
    dma = pltpu.SemaphoreType.DMA
    vmem = pltpu.VMEM
    pairs = lambda n: [dma((n,)), dma((n,))]
    scratch = [
        vmem((160, 256), BF16), vmem((256, 128), BF16), vmem((2, 2, 576, 128), BF16), vmem((512, 1152), BF16),
        vmem((512, 128), BF16), vmem((512, 128), F32), vmem((512, 128), BF16), vmem((128, 1152), BF16),
        vmem((2, NX, NY, HALF, 16, 128), BF16), vmem((2, NY, NX, HALF, 16, 128), BF16),
        vmem((NX, NY, HALF, 16, 128), BF16), vmem((NY, NX, HALF, 16, 128), BF16),
        vmem((3, NY, HALF, 16, 128), BF16), vmem((3, NX, HALF, 16, 128), BF16),
        vmem((NY, HALF, 16, 128), BF16), vmem((NX, HALF, 16, 128), BF16),
        vmem((3, HALF, 16, 128), BF16), vmem((3, HALF, 16, 128), BF16),
        vmem((NZ, 48, 128), BF16), vmem((NZ - 1, 48, 128), BF16),
        vmem((48, 128), F32), vmem((NTM, 48, 128), F32),
    ]
    scratch += pairs(3) + pairs(4) * 2 + pairs(3) * 4 + pairs(7) * 2
    spec = pl.BlockSpec(memory_space=pltpu.VMEM)
    fg, one, two = pl.pallas_call(
        kernel,
        out_shape=(
            jax.ShapeDtypeStruct((64, 256), BF16),
            jax.ShapeDtypeStruct((27, 8, 128), F32),
            jax.ShapeDtypeStruct((27, 4, 128), F32),
        ),
        in_specs=[spec] * 8,
        out_specs=(spec,) * 3,
        scratch_shapes=scratch,
        compiler_params=pltpu.CompilerParams(
            collective_id=0, has_side_effects=True, vmem_limit_bytes=48 * 1024 * 1024
        ),
    )(
        features.reshape(64, 256),
        upstream.reshape(256, 128),
        weight_one.reshape(3, 9, 256, 128),
        weight_two.reshape(3, 9, 128, 128),
        *tables(),
    )
    return (
        fg.reshape(features.shape),
        one.reshape(3, 3, 3, 8, 128),
        two.reshape(3, 3, 3, 4, 128),
    )


def solution(mesh):
    wide = P("dp", "tm", None, None, None)
    cut = P(None, None, None, "dp", None)
    return jax.shard_map(
        on_device, mesh=mesh, in_specs=(wide, wide, P(), P()), out_specs=(wide, cut, cut), check_vma=False
    )
```

time: 477 us -> 58.4 us (0.12)
  waiting for transfers between devices: 392 us -> 0 us
  Pallas kernels: 0 us -> 47.4 us
  blocking collectives: 41.8 us -> 0 us
  between operations: 14.8 us -> 0.66 us
  matrix products: 13.9 us -> 0 us
  starting transfers between devices: 6.87 us -> 0 us
  local copies, waits for them, and re-layouts: 4.21 us -> 9.95 us
    unnamed x4 -> x0, waiting for transfers between devices: 214 us -> none
    psum x1 -> x0, waiting for transfers between devices: 90.8 us -> none  [on_device(): totals = lax.psum((grad_first, grad_second), 'tm')]
    reduce_scatter x1 -> x0, waiting for transfers between devices: 81.7 us -> none  [on_device(): lax.psum_scatter(totals[0], 'dp', scatter_dimension=3, tiled=True)]
    pallas_call x0 -> x1, Pallas kernels: none -> 47.4 us  [on_device(): pl.pallas_call(kernel, out_shape=(jax.ShapeDtypeStruct((64, 256), BF16),...]
    psum x1 -> x0, blocking collectives: 41.8 us -> none  [on_device(): totals = lax.psum((grad_first, grad_second), 'tm')]
    conv_general_dilated x3 -> x0, matrix products: 10.3 us -> none  [the longest x2 8.03 us: kernel_grad(): lax.conv_general_dilated(padded, cotangent, (1, 1, 1), 'VALID', dimension...]
    unnamed x14 -> x19, local copies, waits for them, and re-layouts: 3.09 us -> 9.95 us
    ppermute x3 -> x0, starting transfers between devices: 6.75 us -> none  [passed_along(): return lax.ppermute(value, axis, pairs)]
  transfers between devices with their start and end apart: 6 -> 0, of which waited for: 5 -> 0; matrix products, arithmetic and copies ran while one was open for 4% -> 0% of each run, Pallas kernels for 0% -> 0%
where the time goes in v1:
time: 58.4 us; the launch traced here: 58 us
  Pallas kernels  47.4 us (81%)
  local copies, waits for them, and re-layouts  9.95 us (17%)
  between operations  0.66 us (1%)
    pallas_call x1, Pallas kernels, on_device(): pl.pallas_call(kernel, out_shape=(jax.ShapeDtypeStruct((64, 256), BF16),...  47.4 us
    unnamed x19, local copies, waits for them, and re-layouts  9.95 us

profile of v1, /device:TPU:2, one launch (start us, length us, event | category | flops | bytes accessed | tf_op | source)
XLA Modules:
  0.0 58.0 jit_solution(6043120576871050687)
XLA Ops:
  0.6 0.0 copy-start
  0.6 1.5 %copy-done = bf16[3,3,3,256,128]{4,3,2,1,0:T(8,128)(2,1)S(1)} copy-done((bf16[3,3,3,256,128]{4,3,2,1,0:T(8,128)(2,1)S(1)}, bf16[3,3,3,256,128]{4,3,2,1,0:T(8,128)(2,1)}, u32[]{:S(2)}) %copy-start) | copy-done | bytes 1769496
  2.1 0.0 copy-start.1
  2.1 1.2 %copy-done.1 = bf16[3,3,3,128,128]{4,3,2,1,0:T(8,128)(2,1)S(1)} copy-done((bf16[3,3,3,128,128]{4,3,2,1,0:T(8,128)(2,1)S(1)}, bf16[3,3,3,128,128]{4,3,2,1,0:T(8,128)(2,1)}, u32[]{:S(2)}) %copy-start.1) | copy-done | bytes 884760
  3.3 0.0 copy-start.2
  3.3 1.0 %copy-done.2 = bf16[512,384]{1,0:T(8,128)(2,1)S(1)} copy-done((bf16[512,384]{1,0:T(8,128)(2,1)S(1)}, bf16[512,384]{1,0:T(8,128)(2,1)}, u32[]{:S(2)}) %copy-start.2) | copy-done | bytes 393240
  4.3 0.0 copy-start.3
  4.3 1.0 %copy-done.3 = bf16[256,576]{1,0:T(8,128)(2,1)S(1)} copy-done((bf16[256,576]{1,0:T(8,128)(2,1)S(1)}, bf16[256,576]{1,0:T(8,128)(2,1)}, u32[]{:S(2)}) %copy-start.3) | copy-done | bytes 294936
  5.2 0.0 copy-start.4
  5.2 1.0 %copy-done.4 = bf16[576,256]{1,0:T(8,128)(2,1)S(1)} copy-done((bf16[576,256]{1,0:T(8,128)(2,1)S(1)}, bf16[576,256]{1,0:T(8,128)(2,1)}, u32[]{:S(2)}) %copy-start.4) | copy-done | bytes 294936
  6.2 0.0 copy-start.5
  6.2 0.9 %copy-done.5 = bf16[256,256]{1,0:T(8,128)(2,1)S(1)} copy-done((bf16[256,256]{1,0:T(8,128)(2,1)S(1)}, bf16[256,256]{1,0:T(8,128)(2,1)}, u32[]{:S(2)}) %copy-start.5) | copy-done | bytes 131096
  7.1 0.0 copy-start.6
  7.1 0.8 %copy-done.6 = bf16[1,4,4,16,128]{4,3,2,1,0:T(8,128)(2,1)S(1)} copy-done((bf16[1,4,4,16,128]{4,3,2,1,0:T(8,128)(2,1)S(1)}, bf16[1,4,4,16,128]{4,3,2,1,0:T(8,128)(2,1)}, u32[]{:S(2)}) %copy-start.6) | copy-done | bytes 65560
  8.0 0.0 copy-start.7
  8.0 0.8 %copy-done.7 = bf16[1,4,2,8,256]{4,3,2,1,0:T(8,128)(2,1)S(1)} copy-done((bf16[1,4,2,8,256]{4,3,2,1,0:T(8,128)(2,1)S(1)}, bf16[1,4,2,8,256]{4,3,2,1,0:T(8,128)(2,1)}, u32[]{:S(2)}) %copy-start.7) | copy-done | bytes 32792
  8.7 47.4 %shard_map.103 = (bf16[64,256]{1,0:T(8,128)(2,1)S(1)}, f32[27,8,128]{2,1,0:T(8,128)S(1)}, f32[27,4,128]{2,1,0:T(4,128)S(1)}) custom-call(bf16[64,256]{1,0:T(8,128)(2,1)S(1)} %bitcast.12, bf16[256,128]{1,0:T(8,128)(2,1)S(1)} %bitcast.10, bf16[3,9,256,128]{3,2,1,0:T(8,128)(2,1)S(1)} %bitcast.7, bf16[3,9,128,128]{3,2,1,0:T(8,128)(2,1)S(1)} %bitcast.8, ...), custom_call_target="tpu_custom_call" | custom-call | tf_op jit(solution)/shard_map/pallas_call | solution.py:295
  56.1 0.6 %copy.14 = bf16[1,4,2,8,256]{4,3,2,1,0:T(8,128)(2,1)} copy(bf16[1,4,2,8,256]{4,3,2,1,0:T(8,128)(2,1)S(1)} %bitcast.13) | data formatting | bytes 65536
  56.7 0.6 %copy.15 = f32[3,3,3,8,128]{4,3,2,1,0:T(8,128)} copy(f32[3,3,3,8,128]{4,3,2,1,0:T(8,128)S(1)} %bitcast.9) | data formatting | bytes 221184
  57.4 0.6 %copy.16 = f32[3,3,3,4,128]{4,3,2,1,0:T(4,128)} copy(f32[3,3,3,4,128]{4,3,2,1,0:T(4,128)S(1)} %bitcast.11) | data formatting | bytes 110592
Async XLA Ops:
  0.6 1.5 %copy-start = (bf16[3,3,3,256,128]{4,3,2,1,0:T(8,128)(2,1)S(1)}, bf16[3,3,3,256,128]{4,3,2,1,0:T(8,128)(2,1)}, u32[]{:S(2)}) copy-start(bf16[3,3,3,256,128]{4,3,2,1,0:T(8,128)(2,1)} %param.10) | copy-start | bytes 5308420
  2.1 1.2 %copy-start.1 = (bf16[3,3,3,128,128]{4,3,2,1,0:T(8,128)(2,1)S(1)}, bf16[3,3,3,128,128]{4,3,2,1,0:T(8,128)(2,1)}, u32[]{:S(2)}) copy-start(bf16[3,3,3,128,128]{4,3,2,1,0:T(8,128)(2,1)} %param.11) | copy-start | bytes 2654212
  3.3 1.0 %copy-start.2 = (bf16[512,384]{1,0:T(8,128)(2,1)S(1)}, bf16[512,384]{1,0:T(8,128)(2,1)}, u32[]{:S(2)}) copy-start(bf16[512,384]{1,0:T(8,128)(2,1)} %constant.11.clone.ord2_ref) | copy-start | bytes 1179652
  4.3 1.0 %copy-start.3 = (bf16[256,576]{1,0:T(8,128)(2,1)S(1)}, bf16[256,576]{1,0:T(8,128)(2,1)}, u32[]{:S(2)}) copy-start(bf16[256,576]{1,0:T(8,128)(2,1)} %constant.8.clone.up_ref) | copy-start | bytes 884740
  5.2 1.0 %copy-start.4 = (bf16[576,256]{1,0:T(8,128)(2,1)S(1)}, bf16[576,256]{1,0:T(8,128)(2,1)}, u32[]{:S(2)}) copy-start(bf16[576,256]{1,0:T(8,128)(2,1)} %constant.9.clone.pool_ref) | copy-start | bytes 884740
  6.2 0.9 %copy-start.5 = (bf16[256,256]{1,0:T(8,128)(2,1)S(1)}, bf16[256,256]{1,0:T(8,128)(2,1)}, u32[]{:S(2)}) copy-start(bf16[256,256]{1,0:T(8,128)(2,1)} %constant.10.clone.ord1_ref) | copy-start | bytes 393220
  7.1 0.8 %copy-start.6 = (bf16[1,4,4,16,128]{4,3,2,1,0:T(8,128)(2,1)S(1)}, bf16[1,4,4,16,128]{4,3,2,1,0:T(8,128)(2,1)}, u32[]{:S(2)}) copy-start(bf16[1,4,4,16,128]{4,3,2,1,0:T(8,128)(2,1)} %param.9) | copy-start | bytes 196612
  8.0 0.8 %copy-start.7 = (bf16[1,4,2,8,256]{4,3,2,1,0:T(8,128)(2,1)S(1)}, bf16[1,4,2,8,256]{4,3,2,1,0:T(8,128)(2,1)}, u32[]{:S(2)}) copy-start(bf16[1,4,2,8,256]{4,3,2,1,0:T(8,128)(2,1)} %param.8) | copy-start | bytes 98308

commit v2 on v1

v2 whole, which is shorter than its diff:
```python
import jax
import jax.numpy as jnp
import numpy as np
from jax import lax
from jax.experimental import pallas as pl
from jax.experimental.pallas import tpu as pltpu
from jax.sharding import PartitionSpec as P

MESH = pl.DeviceIdType.MESH
F32, BF16 = jnp.float32, jnp.bfloat16

NZ, NX, NY, NTM = 8, 4, 4, 8


def tables():
    select = np.zeros((256, 576), np.float32)
    for f in range(4):
        for r in range(4):
            for s in range(16):
                for b in range(3):
                    for e in range(3):
                        rr, ss = r + b - 1, s + e - 1
                        if 0 <= rr < 4 and 0 <= ss < 16:
                            select[f * 64 + r * 16 + s, (b * 3 + e) * 64 + f * 16 + rr // 2 * 8 + ss // 2] = 1
    order_one = np.zeros((256, 256), np.float32)
    order_two = np.zeros((512, 384), np.float32)
    for core in range(2):
        for x_lo in range(2):
            for z in range(8):
                d = (core * 2 + x_lo) * 8 + z
                dp = z * 4 + x_lo * 2 + core
                for k in range(8):
                    order_one[d * 8 + k, dp * 8 + k] = 1
                for a in range(3):
                    for k in range(4):
                        order_two[d * 16 + a * 4 + k, a * 128 + dp * 4 + k] = 1
    return [jnp.asarray(m, BF16) for m in (select, select.T, order_one, order_two)]


def dot(a, b):
    return jnp.dot(a, b, preferred_element_type=F32)


def dot_nt(a, b):
    return lax.dot_general(a, b, (((1,), (1,)), ((), ())), preferred_element_type=F32)


def kernel(
    f_hbm, u_hbm, w1_hbm, w2_hbm, up_hbm, pool_hbm, ord1_hbm, ord2_hbm,
    fg_ref, g1_ref, g2_ref,
    u_ref, w1_ref, w2_ref, up_ref, pool_ref, ord1_ref, ord2_ref, s_in,
    fh, uh, um, fm, ystk, u9, u9m, hid, slope, p9, p9m, turned, away, away_in, part, part_in,
    ea, eb, la, lb, ea1, eb1, la1, lb1, sea, seb, sla, slb, ea2, eb2, la2, lb2,
    ze, zl, ze1, zl1, ge, gl, ge_in, gl_in,
    s_near, r_near, s_mate, r_mate,
    s_e1, r_e1, s_l1, r_l1, s_e2, r_e2, s_l2, r_l2, s_e3, r_e3, s_l3, r_l3, s_e4, r_e4, s_l4, r_l4,
):
    tm, dp = lax.axis_index("tm"), lax.axis_index("dp")
    y, x_hi = tm // 2, tm % 2
    z, x_lo, core = dp // 4, (dp // 2) % 2, dp % 2
    x = x_lo * 2 + x_hi

    def at(xx=x, yy=y, zz=z, cc=core):
        return {"tm": yy * 2 + xx % 2, "dp": zz * 4 + (xx // 2) * 2 + cc}

    def at_tm(t):
        return {"tm": t, "dp": dp}

    barrier = pltpu.get_barrier_semaphore()
    peers = [at_tm((tm + k) % NTM) for k in range(1, NTM)]
    peers += [at(zz=(z + k) % NZ) for k in range(1, NZ)]
    peers += [at(cc=1 - core)]
    other = (1 - x_lo) * 2
    peers += [at(xx=other), at(xx=other + 1)]
    for peer in peers:
        pl.semaphore_signal(barrier, inc=1, device_id=peer, device_id_type=MESH)

    loads = []
    order = (
        (u_hbm, u_ref), (f_hbm, fh.at[pl.ds(64, 64)]), (w1_hbm, w1_ref), (up_hbm, up_ref),
        (ord2_hbm, ord2_ref), (w2_hbm, w2_ref), (pool_hbm, pool_ref), (ord1_hbm, ord1_ref),
    )
    for i, (src, dst) in enumerate(order):
        loads.append(pltpu.make_async_copy(src, dst, s_in.at[i]))
        loads[i].start()

    sent = []

    def send(src, dst, ssem, rsem, to):
        copy = pltpu.make_async_remote_copy(
            src_ref=src, dst_ref=dst, send_sem=ssem, recv_sem=rsem, device_id=to, device_id_type=MESH
        )
        copy.start()
        sent.append(copy)
        return copy

    def shifted(block, frames, ref, first):
        n = frames * 64
        column = lax.broadcasted_iota(jnp.int32, (n, 128), 0) % 16
        wide = block.astype(F32)
        back_one = jnp.where(column == 15, 0.0, pltpu.roll(wide, n - 1, 0)).astype(BF16)
        on_one = jnp.where(column == 0, 0.0, pltpu.roll(wide, 1, 0)).astype(BF16)
        zero = jnp.zeros((frames, 16, 128), BF16)
        for e, v in enumerate((back_one, block, on_one)):
            v = v.reshape(frames, 64, 128)
            for b in range(3):
                tap = slice((b * 3 + e) * 128, (b * 3 + e + 1) * 128)
                if b == 0:
                    rows = jnp.concatenate([v[:, 16:], zero], axis=1)
                elif b == 1:
                    rows = v
                else:
                    rows = jnp.concatenate([zero, v[:, :48]], axis=1)
                ref[first : first + n, tap] = rows.reshape(n, 128)

    ystk[...] = jnp.zeros(ystk.shape, BF16)
    p9[0:32, :] = jnp.zeros((32, 1152), BF16)
    p9[96:128, :] = jnp.zeros((32, 1152), BF16)
    loads[0].wait()
    shifted(u_ref[...], 4, u9, 0)

    pl.semaphore_wait(barrier, len(peers))
    nxt, prv, mate = at_tm((tm + 1) % NTM), at_tm((tm + NTM - 1) % NTM), at(cc=1 - core)
    near = [
        send(f_hbm, fh.at[pl.ds(0, 64)], s_near.at[0], r_near.at[0], nxt),
        send(u_hbm.at[pl.ds(0, 128)], uh, s_near.at[1], r_near.at[1], prv),
    ]
    from_mate = [send(u_ref, um, s_mate.at[0], r_mate.at[0], mate)]
    from_mate[0].wait_recv()
    shifted(um[...], 4, u9m, 0)
    for i in range(1, 5):
        loads[i].wait()

    near[0].wait_recv()

    @pl.when(tm == 0)
    def _():
        fh[0:64, :] = jnp.zeros((64, 256), BF16)

    from_mate.append(send(fh.at[pl.ds(32, 96)], fm, s_mate.at[1], r_mate.at[1], mate))
    cat = jnp.concatenate([fh[0:96, :], fh[16:112, :], fh[32:128, :]], axis=1)
    for be in range(9):
        prod = dot(cat, w1_ref[:, be].reshape(768, 128))
        high = prod.astype(BF16)
        low = (prod - high.astype(F32)).astype(BF16)
        ystk[0, 0, be * 64 : be * 64 + 64, :] = high[0:64]
        ystk[0, 1, be * 64 : be * 64 + 64, :] = low[0:64]
        ystk[1, 0, be * 64 : be * 64 + 32, :] = high[64:96]
        ystk[1, 1, be * 64 : be * 64 + 32, :] = low[64:96]
    for blk, n in ((0, 256), (1, 128)):
        pre = dot(up_ref[0:n, :], ystk[blk, 0]) + dot(up_ref[0:n, :], ystk[blk, 1])
        sigma = 1.0 / (1.0 + jnp.exp(-pre))
        hid[blk * 256 : blk * 256 + n, :] = (pre * sigma).astype(BF16)
        slope[blk * 256 : blk * 256 + n, :] = sigma * (1.0 + pre * (1.0 - sigma))

    taps = jnp.concatenate([hid[a * 64 : a * 64 + 256, :] for a in range(3)], axis=1)
    away[...] = dot_nt(ord2_ref[pl.ds(pl.multiple_of((1 - core) * 256, 256), 256), :], taps).astype(BF16)
    from_mate.append(send(away, away_in, s_mate.at[2], r_mate.at[2], mate))
    turned[...] = dot_nt(ord2_ref[pl.ds(pl.multiple_of(core * 256, 256), 256), :], taps).astype(BF16)

    near[1].wait_recv()

    @pl.when(tm == NTM - 1)
    def _():
        uh[...] = jnp.zeros((128, 128), BF16)

    shifted(uh[...], 2, u9, 256)
    for i in range(5, 8):
        loads[i].wait()
    back = jnp.zeros((256, 128), F32)
    for a in range(3):
        kern = jnp.concatenate([w2_ref[a, be] for be in range(9)], axis=1)
        back += dot_nt(u9[(2 - a) * 64 : (2 - a) * 64 + 256, :], kern)
    dpre = (back * slope[128:384, :]).astype(BF16)
    pooled = dot(pool_ref[...], dpre).astype(BF16)
    for be in range(9):
        p9[32:96, be * 128 : be * 128 + 128] = pooled[be * 64 : be * 64 + 64]
    from_mate.append(send(p9.at[pl.ds(32, 64)], p9m, s_mate.at[3], r_mate.at[3], mate))

    def put_late(tile, value):
        value = value.reshape(2, 8, 16, 128)
        for lo in range(2):
            xx, yy = lo * 2 + tile // 2 % 2, tile // 4
            if tile % 2 == 0:
                la[xx, yy] = value[lo]
            else:
                lb[yy, xx] = value[lo]

    from_mate[2].wait_recv()
    for be in range(9):
        tap = slice(be * 128, be * 128 + 128)
        two = dot(turned[...], u9[0:256, tap]) + dot(away_in[...], u9m[:, tap])
        two = two.astype(BF16)
        if be == 8:
            put_late(14, two)
        else:
            two = two.reshape(2, 8, 16, 128)
            for lo in range(2):
                xx, yy = lo * 2 + be % 2, be // 2
                ea[xx, yy] = two[lo, :4]
                eb[yy, xx] = two[lo, 4:]

    def around(src_a, src_b, dst_a, dst_b, ssem, rsem, swap):
        copies = []
        for k in range(1, 4):
            xd, yd = (x + k) % NX, (y + k) % NY
            ia, ib = (yd, xd) if swap else (xd, yd)
            to_a, to_b = (at(yy=yd), at(xx=xd)) if swap else (at(xx=xd), at(yy=yd))
            copies.append(send(src_a.at[ia], dst_a.at[k - 1], ssem.at[2 * k - 2], rsem.at[2 * k - 2], to_a))
            copies.append(send(src_b.at[ib], dst_b.at[k - 1], ssem.at[2 * k - 1], rsem.at[2 * k - 1], to_b))
        return copies

    def added(own, parts, count):
        total = own.astype(F32)
        for k in range(count):
            total += parts[k].astype(F32)
        return total

    e1 = around(ea, eb, ea1, eb1, s_e1, r_e1, False)

    result = jnp.zeros((96, 256), F32)
    for a in range(3):
        kern = jnp.concatenate([w1_ref[a, be] for be in range(9)], axis=1)
        result += dot_nt(p9[(2 - a) * 16 : (2 - a) * 16 + 96, :], kern)
    part[...] = result

    from_mate[1].wait_recv()
    from_mate[3].wait_recv()
    units = []
    pools = jnp.concatenate([p9[32:96, :], p9m[...]], axis=0)
    mine = pl.ds(pl.multiple_of(core * 128, 128), 128)
    for a in range(3):
        rows = jnp.concatenate([fh[32 + a * 16 : 96 + a * 16, :], fm[a * 16 : a * 16 + 64, :]], axis=0)
        feats = dot_nt(ord1_ref[mine, :], rows).astype(BF16)
        for be in range(9):
            units.append(dot(feats, pools[:, be * 128 : be * 128 + 128]).reshape(16, 8, 128))
            if len(units) == 2:
                put_late((a * 9 + be) // 2, jnp.concatenate(units, axis=1).astype(BF16))
                units = []
    units.append(jnp.zeros((16, 8, 128), F32))
    put_late(13, jnp.concatenate(units, axis=1).astype(BF16))
    put_late(15, jnp.zeros((16, 16, 128), BF16))
    l1 = around(la, lb, la1, lb1, s_l1, r_l1, False)
    near.append(send(part.at[pl.ds(0, 32)], part_in, s_near.at[2], r_near.at[2], prv))

    for copy in e1:
        copy.wait_recv()
    sea[...] = added(ea[x], ea1, 3).astype(BF16)
    seb[...] = added(eb[y], eb1, 3).astype(BF16)
    e2 = around(sea, seb, ea2, eb2, s_e2, r_e2, True)
    for copy in l1:
        copy.wait_recv()
    sla[...] = added(la[x], la1, 3).astype(BF16)
    slb[...] = added(lb[y], lb1, 3).astype(BF16)
    l2 = around(sla, slb, la2, lb2, s_l2, r_l2, True)

    def along(src, dst, ssem, rsem):
        copies = []
        for k in range(1, NZ):
            zd = (z + k) % NZ
            copies.append(send(src.at[zd], dst.at[k - 1], ssem.at[k - 1], rsem.at[k - 1], at(zz=zd)))
        return copies

    for copy in e2:
        copy.wait_recv()
    ze[0:4] = added(sea[y], ea2, 3).astype(BF16)
    ze[4:8] = added(seb[x], eb2, 3).astype(BF16)
    e3 = along(ze, ze1, s_e3, r_e3)
    for copy in l2:
        copy.wait_recv()
    zl[:, 0:16] = added(sla[y], la2, 3).astype(BF16)
    zl[:, 16:32] = added(slb[x], lb2, 3).astype(BF16)
    l3 = along(zl, zl1, s_l3, r_l3)

    near[2].wait_recv()
    last = jnp.where(tm == NTM - 1, 0.0, part_in[...])
    fg_ref[0:32, :] = part[32:64, :].astype(BF16)
    fg_ref[32:64, :] = (part[64:96, :] + last).astype(BF16)

    def spread(src, dst, ssem, rsem):
        copies = []
        for k in range(1, NTM):
            to = at_tm((tm + k) % NTM)
            copies.append(send(src, dst.at[tm], ssem.at[k - 1], rsem.at[k - 1], to))
        return copies

    for copy in e3:
        copy.wait_recv()
    ge[...] = added(ze[z], ze1, 7) * (1.0 / 256.0)
    ge_in[tm] = ge[...]
    e4 = spread(ge, ge_in, s_e4, r_e4)
    for copy in l3:
        copy.wait_recv()
    gl[...] = added(zl[z], zl1, 7) * (1.0 / 256.0)
    gl_in[tm] = gl[...]
    l4 = spread(gl, gl_in, s_l4, r_l4)
    for copy in e4:
        copy.wait_recv()
    for be in range(8):
        for a in range(3):
            g2_ref[a * 9 + be] = ge_in[be, a * 4 : a * 4 + 4]
    for copy in l4:
        copy.wait_recv()
    for u in range(27):
        tile, row = u // 2, u % 2 * 8
        row += tile % 2 * 16
        g1_ref[u] = gl_in[tile // 2, row : row + 8]
    for a in range(3):
        g2_ref[a * 9 + 8] = gl_in[7, a * 4 : a * 4 + 4]
    for copy in sent:
        copy.wait_send()


def on_device(features, upstream, weight_one, weight_two):
    dma, vmem = pltpu.SemaphoreType.DMA, pltpu.VMEM
    tile = lambda *lead: vmem(lead + (16, 128), BF16)
    pairs = lambda n: [dma((n,)), dma((n,))]
    scratch = [
        vmem((256, 128), BF16), vmem((3, 9, 256, 128), BF16), vmem((3, 9, 128, 128), BF16),
        vmem((256, 576), BF16), vmem((576, 256), BF16), vmem((256, 256), BF16), vmem((512, 384), BF16), dma((8,)),
        vmem((128, 256), BF16), vmem((128, 128), BF16), vmem((256, 128), BF16), vmem((96, 256), BF16),
        vmem((2, 2, 576, 128), BF16), vmem((384, 1152), BF16), vmem((256, 1152), BF16),
        vmem((384, 128), BF16), vmem((384, 128), F32), vmem((128, 1152), BF16), vmem((64, 1152), BF16),
        vmem((256, 256), BF16), vmem((256, 256), BF16), vmem((256, 256), BF16),
        vmem((96, 256), F32), vmem((32, 256), F32),
        tile(NX, NY, 4), tile(NY, NX, 4), tile(NX, NY, 8), tile(NY, NX, 8),
        tile(3, NY, 4), tile(3, NX, 4), tile(3, NY, 8), tile(3, NX, 8),
        tile(NY, 4), tile(NX, 4), tile(NY, 8), tile(NX, 8),
        tile(3, 4), tile(3, 4), tile(3, 8), tile(3, 8),
        vmem((NZ, 16, 128), BF16), vmem((NZ, 32, 128), BF16), vmem((NZ - 1, 16, 128), BF16), vmem((NZ - 1, 32, 128), BF16),
        vmem((16, 128), F32), vmem((32, 128), F32), vmem((NTM, 16, 128), F32), vmem((NTM, 32, 128), F32),
    ]
    scratch += pairs(3) + pairs(4) + pairs(6) * 4 + pairs(7) * 4
    spec = pl.BlockSpec(memory_space=pltpu.VMEM)
    fg, one, two = pl.pallas_call(
        kernel,
        out_shape=(
            jax.ShapeDtypeStruct((64, 256), BF16),
            jax.ShapeDtypeStruct((27, 8, 128), F32),
            jax.ShapeDtypeStruct((27, 4, 128), F32),
        ),
        in_specs=[pl.BlockSpec(memory_space=pltpu.HBM)] * 8,
        out_specs=(spec,) * 3,
        scratch_shapes=scratch,
        compiler_params=pltpu.CompilerParams(
            collective_id=0, has_side_effects=True, vmem_limit_bytes=24 * 1024 * 1024
        ),
    )(
        *(
            pltpu.with_memory_space_constraint(v, pltpu.HBM)
            for v in (
                features.reshape(64, 256),
                upstream.reshape(256, 128),
                weight_one.reshape(3, 9, 256, 128),
                weight_two.reshape(3, 9, 128, 128),
                *tables(),
            )
        )
    )
    return (
        fg.reshape(features.shape),
        one.reshape(3, 3, 3, 8, 128),
        two.reshape(3, 3, 3, 4, 128),
    )


def solution(mesh):
    wide = P("dp", "tm", None, None, None)
    cut = P(None, None, None, "dp", None)
    return jax.shard_map(
        on_device, mesh=mesh, in_specs=(wide, wide, P(), P()), out_specs=(wide, cut, cut), check_vma=False
    )
```

time: 58.4 us -> 46 us (0.79)
  local copies, waits for them, and re-layouts: 9.95 us -> 1.88 us
  Pallas kernels: 47.4 us -> 43.4 us
    unnamed x19 -> x3, local copies, waits for them, and re-layouts: 9.95 us -> 1.88 us
    pallas_call x1, Pallas kernels: 47.4 us -> 43.4 us  [on_device(): pl.pallas_call(kernel, out_shape=(jax.ShapeDtypeStruct((64, 256), BF16),...]
where the time goes in v2:
time: 46 us; the launch traced here: 45.9 us
  Pallas kernels  43.4 us (94%)
  local copies, waits for them, and re-layouts  1.88 us (4%)
  between operations  0.64 us (1%)
    pallas_call x1, Pallas kernels, on_device(): pl.pallas_call(kernel, out_shape=(jax.ShapeDtypeStruct((64, 256), BF16),...  43.4 us
    unnamed x3, local copies, waits for them, and re-layouts  1.88 us

profile of v2, /device:TPU:2, one launch (start us, length us, event | category | flops | bytes accessed | tf_op | source)
XLA Modules:
  0.0 45.9 jit_solution(3577786023444926404)
XLA Ops:
  0.6 43.4 %shard_map.103 = (bf16[64,256]{1,0:T(8,128)(2,1)S(1)}, f32[27,8,128]{2,1,0:T(8,128)S(1)}, f32[27,4,128]{2,1,0:T(4,128)S(1)}) custom-call(bf16[64,256]{1,0:T(8,128)(2,1)} %bitcast.13, bf16[256,128]{1,0:T(8,128)(2,1)} %bitcast.12, bf16[3,9,256,128]{3,2,1,0:T(8,128)(2,1)} %bitcast.10, bf16[3,9,128,128]{3,2,1,0:T(8,128)(2,1)} %bitcast.11, ...), custom_call_target="tpu_custom_call" | custom-call | tf_op jit(solution)/shard_map/pallas_call | solution.py:335
  44.0 0.6 %copy.14 = bf16[1,4,2,8,256]{4,3,2,1,0:T(8,128)(2,1)} copy(bf16[1,4,2,8,256]{4,3,2,1,0:T(8,128)(2,1)S(1)} %bitcast.9) | data formatting | bytes 65536
  44.6 0.6 %copy.15 = f32[3,3,3,8,128]{4,3,2,1,0:T(8,128)} copy(f32[3,3,3,8,128]{4,3,2,1,0:T(8,128)S(1)} %bitcast.7) | data formatting | bytes 221184
  45.3 0.6 %copy.16 = f32[3,3,3,4,128]{4,3,2,1,0:T(4,128)} copy(f32[3,3,3,4,128]{4,3,2,1,0:T(4,128)S(1)} %bitcast.8) | data formatting | bytes 110592

commit v3 on v2

--- a/solution.py
+++ b/solution.py
@@ -49,7 +49,7 @@
     f_hbm, u_hbm, w1_hbm, w2_hbm, up_hbm, pool_hbm, ord1_hbm, ord2_hbm,
     fg_ref, g1_ref, g2_ref,
     u_ref, w1_ref, w2_ref, up_ref, pool_ref, ord1_ref, ord2_ref, s_in,
-    fh, uh, um, fm, ystk, u9, u9m, hid, slope, p9, p9m, turned, away, away_in, part, part_in,
+    fh, uh, um, uhm, fm, fz, ystk, ycor, u9, u9m, hid, pre_ref, back_ref, slope, p9, p9m, turned, away, away_in, part, part_in,
     ea, eb, la, lb, ea1, eb1, la1, lb1, sea, seb, sla, slb, ea2, eb2, la2, lb2,
     ze, zl, ze1, zl1, ge, gl, ge_in, gl_in,
     s_near, r_near, s_mate, r_mate,
@@ -77,7 +77,7 @@
 
     loads = []
     order = (
-        (u_hbm, u_ref), (f_hbm, fh.at[pl.ds(64, 64)]), (w1_hbm, w1_ref), (up_hbm, up_ref),
+        (u_hbm, u_ref), (f_hbm, fh.at[pl.ds(32, 64)]), (w1_hbm, w1_ref), (up_hbm, up_ref),
         (ord2_hbm, ord2_ref), (w2_hbm, w2_ref), (pool_hbm, pool_ref), (ord1_hbm, ord1_ref),
     )
     for i, (src, dst) in enumerate(order):
@@ -113,50 +113,77 @@
                     rows = jnp.concatenate([zero, v[:, :48]], axis=1)
                 ref[first : first + n, tap] = rows.reshape(n, 128)
 
-    ystk[...] = jnp.zeros(ystk.shape, BF16)
+    def gate(pre, rows):
+        sigma = 1.0 / (1.0 + jnp.exp(-pre))
+        hid[128 + rows.start : 128 + rows.stop, :] = (pre * sigma).astype(BF16)
+        slope[rows, :] = sigma * (1.0 + pre * (1.0 - sigma))
+
+    def halves(value):
+        high = value.astype(BF16)
+        return high, (value - high.astype(F32)).astype(BF16)
+
+    def conv_kern(a):
+        return jnp.concatenate([w2_ref[a, be] for be in range(9)], axis=1)
+
+    ycor[...] = jnp.zeros(ycor.shape, BF16)
+    hid[0:128, :] = jnp.zeros((128, 128), BF16)
+    hid[384:512, :] = jnp.zeros((128, 128), BF16)
+    u9[256:384, :] = jnp.zeros((128, 1152), BF16)
     p9[0:32, :] = jnp.zeros((32, 1152), BF16)
     p9[96:128, :] = jnp.zeros((32, 1152), BF16)
     loads[0].wait()
     shifted(u_ref[...], 4, u9, 0)
+    loads[1].wait()
 
     pl.semaphore_wait(barrier, len(peers))
     nxt, prv, mate = at_tm((tm + 1) % NTM), at_tm((tm + NTM - 1) % NTM), at(cc=1 - core)
     near = [
-        send(f_hbm, fh.at[pl.ds(0, 64)], s_near.at[0], r_near.at[0], nxt),
-        send(u_hbm.at[pl.ds(0, 128)], uh, s_near.at[1], r_near.at[1], prv),
+        send(fh.at[pl.ds(64, 32)], fh.at[pl.ds(0, 32)], s_near.at[0], r_near.at[0], nxt),
+        send(u_ref.at[pl.ds(0, 128)], uh, s_near.at[1], r_near.at[1], prv),
     ]
-    from_mate = [send(u_ref, um, s_mate.at[0], r_mate.at[0], mate)]
+    from_mate = [
+        send(u_ref, um, s_mate.at[0], r_mate.at[0], mate),
+        send(fh.at[pl.ds(32, 64)], fm.at[pl.ds(32, 64)], s_mate.at[1], r_mate.at[1], mate),
+    ]
+
+    for i in range(2, 4):
+        loads[i].wait()
+    fz[0:32, :] = jnp.zeros((32, 256), BF16)
+    fz[32:96, :] = fh[32:96, :]
+    cat = jnp.concatenate([fz[0:64, :], fz[16:80, :], fz[32:96, :]], axis=1)
+    for be in range(9):
+        rows = slice(be * 64, be * 64 + 64)
+        ystk[0, rows, :], ystk[1, rows, :] = halves(dot(cat, w1_ref[:, be].reshape(768, 128)))
+    pre = dot(up_ref[...], ystk[0]) + dot(up_ref[...], ystk[1])
+    pre_ref[...] = pre[0:128]
+    gate(pre[128:256], slice(128, 256))
+    for i in range(4, 8):
+        loads[i].wait()
+    back = jnp.zeros((256, 128), F32)
+    for a in range(3):
+        back += dot_nt(u9[(2 - a) * 64 : (2 - a) * 64 + 256, :], conv_kern(a))
+    back_ref[...] = back
     from_mate[0].wait_recv()
     shifted(um[...], 4, u9m, 0)
-    for i in range(1, 5):
-        loads[i].wait()
 
     near[0].wait_recv()
 
     @pl.when(tm == 0)
     def _():
-        fh[0:64, :] = jnp.zeros((64, 256), BF16)
-
-    from_mate.append(send(fh.at[pl.ds(32, 96)], fm, s_mate.at[1], r_mate.at[1], mate))
-    cat = jnp.concatenate([fh[0:96, :], fh[16:112, :], fh[32:128, :]], axis=1)
+        fh[0:32, :] = jnp.zeros((32, 256), BF16)
+
+    from_mate.append(send(fh.at[pl.ds(0, 32)], fm.at[pl.ds(0, 32)], s_mate.at[2], r_mate.at[2], mate))
+    one = jnp.concatenate([fh[0:16, :], fh[16:32, :]], axis=1)
+    two = jnp.concatenate([fh[16:32, :], jnp.zeros((16, 256), BF16)], axis=1)
+    cat = jnp.concatenate([one, two], axis=0)
     for be in range(9):
-        prod = dot(cat, w1_ref[:, be].reshape(768, 128))
-        high = prod.astype(BF16)
-        low = (prod - high.astype(F32)).astype(BF16)
-        ystk[0, 0, be * 64 : be * 64 + 64, :] = high[0:64]
-        ystk[0, 1, be * 64 : be * 64 + 64, :] = low[0:64]
-        ystk[1, 0, be * 64 : be * 64 + 32, :] = high[64:96]
-        ystk[1, 1, be * 64 : be * 64 + 32, :] = low[64:96]
-    for blk, n in ((0, 256), (1, 128)):
-        pre = dot(up_ref[0:n, :], ystk[blk, 0]) + dot(up_ref[0:n, :], ystk[blk, 1])
-        sigma = 1.0 / (1.0 + jnp.exp(-pre))
-        hid[blk * 256 : blk * 256 + n, :] = (pre * sigma).astype(BF16)
-        slope[blk * 256 : blk * 256 + n, :] = sigma * (1.0 + pre * (1.0 - sigma))
-
-    taps = jnp.concatenate([hid[a * 64 : a * 64 + 256, :] for a in range(3)], axis=1)
+        rows = slice(be * 64, be * 64 + 32)
+        ycor[0, rows, :], ycor[1, rows, :] = halves(dot(cat, w1_ref[0:2, be].reshape(512, 128)))
+    gate(pre_ref[...] + (dot(up_ref[0:128, :], ycor[0]) + dot(up_ref[0:128, :], ycor[1])), slice(0, 128))
+
+    taps = jnp.concatenate([hid[a * 64 : a * 64 + 384, :] for a in range(3)], axis=1)
     away[...] = dot_nt(ord2_ref[pl.ds(pl.multiple_of((1 - core) * 256, 256), 256), :], taps).astype(BF16)
-    from_mate.append(send(away, away_in, s_mate.at[2], r_mate.at[2], mate))
-    turned[...] = dot_nt(ord2_ref[pl.ds(pl.multiple_of(core * 256, 256), 256), :], taps).astype(BF16)
+    from_mate.append(send(away, away_in, s_mate.at[3], r_mate.at[3], mate))
 
     near[1].wait_recv()
 
@@ -164,18 +191,18 @@
     def _():
         uh[...] = jnp.zeros((128, 128), BF16)
 
+    from_mate.append(send(uh, uhm, s_mate.at[4], r_mate.at[4], mate))
     shifted(uh[...], 2, u9, 256)
-    for i in range(5, 8):
-        loads[i].wait()
-    back = jnp.zeros((256, 128), F32)
-    for a in range(3):
-        kern = jnp.concatenate([w2_ref[a, be] for be in range(9)], axis=1)
-        back += dot_nt(u9[(2 - a) * 64 : (2 - a) * 64 + 256, :], kern)
-    dpre = (back * slope[128:384, :]).astype(BF16)
+    later = dot_nt(u9[256:384, :], conv_kern(0))
+    third = jnp.concatenate([jnp.zeros((64, 1152), BF16), u9[256:320, :]], axis=0)
+    later += dot_nt(third, conv_kern(1))
+    back_ref[128:256, :] += later
+    dpre = (back_ref[...] * slope[...]).astype(BF16)
     pooled = dot(pool_ref[...], dpre).astype(BF16)
     for be in range(9):
         p9[32:96, be * 128 : be * 128 + 128] = pooled[be * 64 : be * 64 + 64]
-    from_mate.append(send(p9.at[pl.ds(32, 64)], p9m, s_mate.at[3], r_mate.at[3], mate))
+    from_mate.append(send(p9.at[pl.ds(32, 64)], p9m, s_mate.at[5], r_mate.at[5], mate))
+    turned[...] = dot_nt(ord2_ref[pl.ds(pl.multiple_of(core * 256, 256), 256), :], taps).astype(BF16)
 
     def put_late(tile, value):
         value = value.reshape(2, 8, 16, 128)
@@ -186,10 +213,12 @@
             else:
                 lb[yy, xx] = value[lo]
 
-    from_mate[2].wait_recv()
+    from_mate[4].wait_recv()
+    shifted(uhm[...], 2, u9m, 256)
+    from_mate[3].wait_recv()
     for be in range(9):
         tap = slice(be * 128, be * 128 + 128)
-        two = dot(turned[...], u9[0:256, tap]) + dot(away_in[...], u9m[:, tap])
+        two = dot(turned[...], u9[:, tap]) + dot(away_in[...], u9m[:, tap])
         two = two.astype(BF16)
         if be == 8:
             put_late(14, two)
@@ -218,22 +247,19 @@
 
     e1 = around(ea, eb, ea1, eb1, s_e1, r_e1, False)
 
-    result = jnp.zeros((96, 256), F32)
+    from_mate[1].wait_recv()
+    from_mate[2].wait_recv()
+    feats = []
+    mine = pl.ds(pl.multiple_of(core * 128, 128), 128)
     for a in range(3):
-        kern = jnp.concatenate([w1_ref[a, be] for be in range(9)], axis=1)
-        result += dot_nt(p9[(2 - a) * 16 : (2 - a) * 16 + 96, :], kern)
-    part[...] = result
-
-    from_mate[1].wait_recv()
-    from_mate[3].wait_recv()
+        rows = jnp.concatenate([fh[a * 16 : a * 16 + 64, :], fm[a * 16 : a * 16 + 64, :]], axis=0)
+        feats.append(dot_nt(ord1_ref[mine, :], rows).astype(BF16))
+    from_mate[5].wait_recv()
     units = []
     pools = jnp.concatenate([p9[32:96, :], p9m[...]], axis=0)
-    mine = pl.ds(pl.multiple_of(core * 128, 128), 128)
     for a in range(3):
-        rows = jnp.concatenate([fh[32 + a * 16 : 96 + a * 16, :], fm[a * 16 : a * 16 + 64, :]], axis=0)
-        feats = dot_nt(ord1_ref[mine, :], rows).astype(BF16)
         for be in range(9):
-            units.append(dot(feats, pools[:, be * 128 : be * 128 + 128]).reshape(16, 8, 128))
+            units.append(dot(feats[a], pools[:, be * 128 : be * 128 + 128]).reshape(16, 8, 128))
             if len(units) == 2:
                 put_late((a * 9 + be) // 2, jnp.concatenate(units, axis=1).astype(BF16))
                 units = []
@@ -241,6 +267,11 @@
     put_late(13, jnp.concatenate(units, axis=1).astype(BF16))
     put_late(15, jnp.zeros((16, 16, 128), BF16))
     l1 = around(la, lb, la1, lb1, s_l1, r_l1, False)
+    result = jnp.zeros((96, 256), F32)
+    for a in range(3):
+        kern = jnp.concatenate([w1_ref[a, be] for be in range(9)], axis=1)
+        result += dot_nt(p9[(2 - a) * 16 : (2 - a) * 16 + 96, :], kern)
+    part[...] = result
     near.append(send(part.at[pl.ds(0, 32)], part_in, s_near.at[2], r_near.at[2], prv))
 
     for copy in e1:
@@ -286,29 +317,43 @@
 
     for copy in e3:
         copy.wait_recv()
-    ge[...] = added(ze[z], ze1, 7) * (1.0 / 256.0)
+    ge[...] = added(ze[z], ze1, 7).astype(BF16)
     ge_in[tm] = ge[...]
     e4 = spread(ge, ge_in, s_e4, r_e4)
     for copy in l3:
         copy.wait_recv()
-    gl[...] = added(zl[z], zl1, 7) * (1.0 / 256.0)
+    gl[...] = added(zl[z], zl1, 7).astype(BF16)
     gl_in[tm] = gl[...]
     l4 = spread(gl, gl_in, s_l4, r_l4)
     for copy in e4:
         copy.wait_recv()
+    factor = 1.0 / 256.0
     for be in range(8):
+        rows = ge_in[be].astype(F32) * factor
         for a in range(3):
-            g2_ref[a * 9 + be] = ge_in[be, a * 4 : a * 4 + 4]
+            g2_ref[a * 9 + be] = rows[a * 4 : a * 4 + 4]
     for copy in l4:
         copy.wait_recv()
-    for u in range(27):
-        tile, row = u // 2, u % 2 * 8
-        row += tile % 2 * 16
-        g1_ref[u] = gl_in[tile // 2, row : row + 8]
-    for a in range(3):
-        g2_ref[a * 9 + 8] = gl_in[7, a * 4 : a * 4 + 4]
+    for tile in range(15):
+        rows = gl_in[tile // 2, tile % 2 * 16 : tile % 2 * 16 + 16, :].astype(F32) * factor
+        if tile < 14:
+            g1_ref[2 * tile] = rows[0:8]
+        if tile < 13:
+            g1_ref[2 * tile + 1] = rows[8:16]
+        if tile == 14:
+            for a in range(3):
+                g2_ref[a * 9 + 8] = rows[a * 4 : a * 4 + 4]
     for copy in sent:
         copy.wait_send()
+
+
+def store(*refs):
+    sems = refs[6]
+    copies = [pltpu.make_async_copy(refs[i], refs[3 + i], sems.at[i]) for i in range(3)]
+    for copy in copies:
+        copy.start()
+    for copy in copies:
+        copy.wait()
 
 
 def on_device(features, upstream, weight_one, weight_two):
@@ -318,27 +363,30 @@
     scratch = [
         vmem((256, 128), BF16), vmem((3, 9, 256, 128), BF16), vmem((3, 9, 128, 128), BF16),
         vmem((256, 576), BF16), vmem((576, 256), BF16), vmem((256, 256), BF16), vmem((512, 384), BF16), dma((8,)),
-        vmem((128, 256), BF16), vmem((128, 128), BF16), vmem((256, 128), BF16), vmem((96, 256), BF16),
-        vmem((2, 2, 576, 128), BF16), vmem((384, 1152), BF16), vmem((256, 1152), BF16),
-        vmem((384, 128), BF16), vmem((384, 128), F32), vmem((128, 1152), BF16), vmem((64, 1152), BF16),
-        vmem((256, 256), BF16), vmem((256, 256), BF16), vmem((256, 256), BF16),
+        vmem((96, 256), BF16), vmem((128, 128), BF16), vmem((256, 128), BF16), vmem((128, 128), BF16),
+        vmem((96, 256), BF16), vmem((96, 256), BF16),
+        vmem((2, 576, 128), BF16), vmem((2, 576, 128), BF16), vmem((384, 1152), BF16), vmem((384, 1152), BF16),
+        vmem((512, 128), BF16), vmem((128, 128), F32), vmem((256, 128), F32), vmem((256, 128), F32),
+        vmem((128, 1152), BF16), vmem((64, 1152), BF16),
+        vmem((256, 384), BF16), vmem((256, 384), BF16), vmem((256, 384), BF16),
         vmem((96, 256), F32), vmem((32, 256), F32),
         tile(NX, NY, 4), tile(NY, NX, 4), tile(NX, NY, 8), tile(NY, NX, 8),
         tile(3, NY, 4), tile(3, NX, 4), tile(3, NY, 8), tile(3, NX, 8),
         tile(NY, 4), tile(NX, 4), tile(NY, 8), tile(NX, 8),
         tile(3, 4), tile(3, 4), tile(3, 8), tile(3, 8),
         vmem((NZ, 16, 128), BF16), vmem((NZ, 32, 128), BF16), vmem((NZ - 1, 16, 128), BF16), vmem((NZ - 1, 32, 128), BF16),
-        vmem((16, 128), F32), vmem((32, 128), F32), vmem((NTM, 16, 128), F32), vmem((NTM, 32, 128), F32),
+        vmem((16, 128), BF16), vmem((32, 128), BF16), vmem((NTM, 16, 128), BF16), vmem((NTM, 32, 128), BF16),
     ]
-    scratch += pairs(3) + pairs(4) + pairs(6) * 4 + pairs(7) * 4
+    scratch += pairs(3) + pairs(6) + pairs(6) * 4 + pairs(7) * 4
     spec = pl.BlockSpec(memory_space=pltpu.VMEM)
-    fg, one, two = pl.pallas_call(
+    shapes = (
+        jax.ShapeDtypeStruct((64, 256), BF16),
+        jax.ShapeDtypeStruct((27, 8, 128), F32),
+        jax.ShapeDtypeStruct((27, 4, 128), F32),
+    )
+    results = pl.pallas_call(
         kernel,
-        out_shape=(
-            jax.ShapeDtypeStruct((64, 256), BF16),
-            jax.ShapeDtypeStruct((27, 8, 128), F32),
-            jax.ShapeDtypeStruct((27, 4, 128), F32),
-        ),
+        out_shape=shapes,
         in_specs=[pl.BlockSpec(memory_space=pltpu.HBM)] * 8,
         out_specs=(spec,) * 3,
         scratch_shapes=scratch,
@@ -357,6 +405,13 @@
             )
         )
     )
+    fg, one, two = pl.pallas_call(
+        store,
+        out_shape=shapes,
+        in_specs=[spec] * 3,
+        out_specs=(pl.BlockSpec(memory_space=pltpu.HBM),) * 3,
+        scratch_shapes=[dma((3,))],
+    )(*(pltpu.with_memory_space_constraint(v, pltpu.VMEM) for v in results))
     return (
         fg.reshape(features.shape),
         one.reshape(3, 3, 3, 8, 128),

time: 46 us -> 44.3 us (0.963)
  local copies, waits for them, and re-layouts: 1.88 us -> 0 us
    unnamed x3 -> x0, local copies, waits for them, and re-layouts: 1.88 us -> none
    pallas_call x1 -> x2, Pallas kernels: 43.4 us -> 43.6 us  [the longest x1 42.9 us: on_device(): pl.pallas_call(kernel, out_shape=shapes, in_specs=[pl.BlockSpec(memory_sp...]
where the time goes in v3:
time: 44.3 us; the launch traced here: 44.2 us
  Pallas kernels  43.6 us (98%)
  between operations  0.64 us (1%)
    pallas_call x1, Pallas kernels, on_device(): pl.pallas_call(kernel, out_shape=shapes, in_specs=[pl.BlockSpec(memory_sp...  42.9 us

profile of v3, /device:TPU:2, one launch (start us, length us, event | category | flops | bytes accessed | tf_op | source)
XLA Modules:
  0.0 44.2 jit_solution(517342679251646177)
XLA Ops:
  0.6 42.9 %shard_map.103 = (bf16[64,256]{1,0:T(8,128)(2,1)S(1)}, f32[27,8,128]{2,1,0:T(8,128)S(1)}, f32[27,4,128]{2,1,0:T(4,128)S(1)}) custom-call(bf16[64,256]{1,0:T(8,128)(2,1)} %bitcast.10, bf16[256,128]{1,0:T(8,128)(2,1)} %bitcast.9, bf16[3,9,256,128]{3,2,1,0:T(8,128)(2,1)} %bitcast.7, bf16[3,9,128,128]{3,2,1,0:T(8,128)(2,1)} %bitcast.8, ...), custom_call_target="tpu_custom_call" | custom-call | tf_op jit(solution)/shard_map/pallas_call | solution.py:387
  43.5 0.7 %shard_map.104 = (bf16[64,256]{1,0:T(8,128)(2,1)}, f32[27,8,128]{2,1,0:T(8,128)}, f32[27,4,128]{2,1,0:T(4,128)}) custom-call(bf16[64,256]{1,0:T(8,128)(2,1)S(1)} %get-tuple-element.9.refs_0_, f32[27,8,128]{2,1,0:T(8,128)S(1)} %get-tuple-element.10.refs_1_, f32[27,4,128]{2,1,0:T(4,128)S(1)} %get-tuple-element.11.refs_2_), custom_call_target="tpu_custom_call" | custom-call | tf_op jit(solution)/shard_map/pallas_call | solution.py:408

commit v4 on v3

v4 whole, which is shorter than its diff:
```python
import jax
import jax.numpy as jnp
import numpy as np
from jax import lax
from jax.experimental import pallas as pl
from jax.experimental.pallas import tpu as pltpu
from jax.sharding import PartitionSpec as P

MESH = pl.DeviceIdType.MESH
F32, BF16 = jnp.float32, jnp.bfloat16

NZ, NX, NY, NTM = 8, 4, 4, 8
CUT = 5


def tables():
    select = np.zeros((256, 576), np.float32)
    for f in range(4):
        for r in range(4):
            for s in range(16):
                for b in range(3):
                    for e in range(3):
                        rr, ss = r + b - 1, s + e - 1
                        if 0 <= rr < 4 and 0 <= ss < 16:
                            select[f * 64 + r * 16 + s, (b * 3 + e) * 64 + f * 16 + rr // 2 * 8 + ss // 2] = 1
    order_one = np.zeros((256, 256), np.float32)
    order_two = np.zeros((512, 384), np.float32)
    for core in range(2):
        for x_lo in range(2):
            for z in range(8):
                d = (core * 2 + x_lo) * 8 + z
                dp = z * 4 + x_lo * 2 + core
                for k in range(8):
                    order_one[d * 8 + k, dp * 8 + k] = 1
                for a in range(3):
                    for k in range(4):
                        order_two[d * 16 + a * 4 + k, a * 128 + dp * 4 + k] = 1
    return [jnp.asarray(m, BF16) for m in (select, select.T, order_one, order_two)]


def dot(a, b):
    return jnp.dot(a, b, preferred_element_type=F32)


def dot_nt(a, b):
    return lax.dot_general(a, b, (((1,), (1,)), ((), ())), preferred_element_type=F32)


def kernel(
    f_hbm, u_hbm, w1_hbm, w2_hbm, up_hbm, pool_hbm, ord1_hbm, ord2_hbm,
    fg_ref, g1_ref, g2_ref,
    u_ref, w1_ref, w2_ref, up_ref, pool_ref, ord1_ref, ord2_ref, s_in,
    fh, uh, um, uhm, fm, fz, ystk, ycor, u9, u9m, hid, pre_ref, back_ref, slope, p9, p9m, turned, away, away_in, part, part_in,
    sum_a, sum_b, in_a, in_b, mid_a, mid_b, mid_in_a, mid_in_b, last, last_in, own, gath,
    final, c_sum, c_in, c_mid, c_mid_in, c_end, c_end_in, d_sum, d_in, d_mid, d_mid_in, d_end, d_end_in,
    s_near, r_near, s_mate, r_mate, s_one, r_one, s_two, r_two, s_three, r_three, s_four, r_four,
    s_c1, r_c1, s_c2, r_c2, s_c3, r_c3, s_d1, r_d1, s_d2, r_d2, s_d3, r_d3,
):
    tm, dp = lax.axis_index("tm"), lax.axis_index("dp")
    y, x_hi = tm // 2, tm % 2
    z, x_lo, core = dp // 4, (dp // 2) % 2, dp % 2
    x = x_lo * 2 + x_hi

    def at(xx=x, yy=y, zz=z, cc=core):
        return {"tm": yy * 2 + xx % 2, "dp": zz * 4 + (xx // 2) * 2 + cc}

    def at_tm(t):
        return {"tm": t, "dp": dp}

    barrier = pltpu.get_barrier_semaphore()
    peers = [at_tm((tm + k) % NTM) for k in range(1, NTM)]
    peers += [at(zz=(z + k) % NZ) for k in range(1, NZ)]
    peers += [at(cc=1 - core)]
    other = (1 - x_lo) * 2
    peers += [at(xx=other), at(xx=other + 1)]
    for peer in peers:
        pl.semaphore_signal(barrier, inc=1, device_id=peer, device_id_type=MESH)

    loads = []
    order = (
        (u_hbm, u_ref), (f_hbm, fh.at[pl.ds(32, 64)]), (up_hbm, up_ref),
        (ord2_hbm, ord2_ref), (pool_hbm, pool_ref), (ord1_hbm, ord1_ref),
    )
    for i, (src, dst) in enumerate(order):
        loads.append(pltpu.make_async_copy(src, dst, s_in.at[i]))
    one, two = [], []
    for be in range(9):
        tap = pl.ds(be * 128, 128)
        one.append(pltpu.make_async_copy(w1_hbm.at[:, be], w1_ref.at[:, :, tap], s_in.at[6 + be]))
        two.append(pltpu.make_async_copy(w2_hbm.at[:, be], w2_ref.at[:, :, tap], s_in.at[15 + be]))
    for copy in loads[:2] + one + loads[2:3] + two + loads[3:]:
        copy.start()

    sent = []

    def send(src, dst, ssem, rsem, to):
        copy = pltpu.make_async_remote_copy(
            src_ref=src, dst_ref=dst, send_sem=ssem, recv_sem=rsem, device_id=to, device_id_type=MESH
        )
        copy.start()
        sent.append(copy)
        return copy

    def shifted(block, frames, ref, first):
        n = frames * 64
        column = lax.broadcasted_iota(jnp.int32, (n, 128), 0) % 16
        wide = block.astype(F32)
        back_one = jnp.where(column == 15, 0.0, pltpu.roll(wide, n - 1, 0)).astype(BF16)
        on_one = jnp.where(column == 0, 0.0, pltpu.roll(wide, 1, 0)).astype(BF16)
        zero = jnp.zeros((frames, 16, 128), BF16)
        for e, v in enumerate((back_one, block, on_one)):
            v = v.reshape(frames, 64, 128)
            for b in range(3):
                tap = slice((b * 3 + e) * 128, (b * 3 + e + 1) * 128)
                if b == 0:
                    rows = jnp.concatenate([v[:, 16:], zero], axis=1)
                elif b == 1:
                    rows = v
                else:
                    rows = jnp.concatenate([zero, v[:, :48]], axis=1)
                ref[first : first + n, tap] = rows.reshape(n, 128)

    def gate(pre, rows):
        sigma = 1.0 / (1.0 + jnp.exp(-pre))
        hid[128 + rows.start : 128 + rows.stop, :] = (pre * sigma).astype(BF16)
        slope[rows, :] = sigma * (1.0 + pre * (1.0 - sigma))

    def halves(value):
        high = value.astype(BF16)
        return high, (value - high.astype(F32)).astype(BF16)

    def keep_halves(value, ref):
        high, low = halves(value)
        n = value.shape[0]
        for be in range(9):
            tap, rows = slice(be * 128, be * 128 + 128), slice(be * 64, be * 64 + n)
            ref[rows, 0:128] = high[:, tap]
            ref[rows, 128:256] = low[:, tap]

    def widened(rows, ref):
        both = dot(up_ref[0:rows, :], ref[...])
        return both[:, 0:128] + both[:, 128:256]

    ycor[...] = jnp.zeros(ycor.shape, BF16)
    hid[0:128, :] = jnp.zeros((128, 128), BF16)
    hid[384:512, :] = jnp.zeros((128, 128), BF16)
    u9[256:384, :] = jnp.zeros((128, 1152), BF16)
    p9[0:32, :] = jnp.zeros((32, 1152), BF16)
    p9[96:128, :] = jnp.zeros((32, 1152), BF16)
    loads[0].wait()
    shifted(u_ref[...], 4, u9, 0)
    loads[1].wait()

    pl.semaphore_wait(barrier, len(peers))
    nxt, prv, mate = at_tm((tm + 1) % NTM), at_tm((tm + NTM - 1) % NTM), at(cc=1 - core)
    near = [
        send(fh.at[pl.ds(64, 32)], fh.at[pl.ds(0, 32)], s_near.at[0], r_near.at[0], nxt),
        send(u_ref.at[pl.ds(0, 128)], uh, s_near.at[1], r_near.at[1], prv),
    ]
    from_mate = [
        send(u_ref, um, s_mate.at[0], r_mate.at[0], mate),
        send(fh.at[pl.ds(32, 64)], fm.at[pl.ds(32, 64)], s_mate.at[1], r_mate.at[1], mate),
    ]

    for copy in one + loads[2:3]:
        copy.wait()
    fz[0:32, :] = jnp.zeros((32, 256), BF16)
    fz[32:96, :] = fh[32:96, :]
    cat = jnp.concatenate([fz[0:64, :], fz[16:80, :], fz[32:96, :]], axis=1)
    keep_halves(dot(cat, w1_ref[...].reshape(768, 1152)), ystk)
    pre = widened(256, ystk)
    pre_ref[...] = pre[0:128]
    gate(pre[128:256], slice(128, 256))
    for copy in two + loads[3:]:
        copy.wait()
    back = jnp.zeros((256, 128), F32)
    for a in range(3):
        back += dot_nt(u9[(2 - a) * 64 : (2 - a) * 64 + 256, :], w2_ref[a])
    back_ref[...] = back
    from_mate[0].wait_recv()
    shifted(um[...], 4, u9m, 0)

    near[0].wait_recv()

    @pl.when(tm == 0)
    def _():
        fh[0:32, :] = jnp.zeros((32, 256), BF16)

    from_mate.append(send(fh.at[pl.ds(0, 32)], fm.at[pl.ds(0, 32)], s_mate.at[2], r_mate.at[2], mate))
    head = jnp.concatenate([fh[0:16, :], fh[16:32, :]], axis=1)
    tail = jnp.concatenate([fh[16:32, :], jnp.zeros((16, 256), BF16)], axis=1)
    cat = jnp.concatenate([head, tail], axis=0)
    keep_halves(dot(cat, w1_ref[0:2].reshape(512, 1152)), ycor)
    gate(pre_ref[...] + widened(128, ycor), slice(0, 128))

    taps = jnp.concatenate([hid[a * 64 : a * 64 + 384, :] for a in range(3)], axis=1)
    away[...] = dot_nt(ord2_ref[pl.ds(pl.multiple_of((1 - core) * 256, 256), 256), :], taps).astype(BF16)
    from_mate.append(send(away, away_in, s_mate.at[3], r_mate.at[3], mate))

    near[1].wait_recv()

    @pl.when(tm == NTM - 1)
    def _():
        uh[...] = jnp.zeros((128, 128), BF16)

    from_mate.append(send(uh, uhm, s_mate.at[4], r_mate.at[4], mate))
    shifted(uh[...], 2, u9, 256)
    later = dot_nt(u9[256:384, :], w2_ref[0:2].reshape(256, 1152))
    back_ref[128:256, :] += later[:, 0:128]
    back_ref[192:256, :] += later[0:64, 128:256]
    dpre = (back_ref[...] * slope[...]).astype(BF16)
    pooled = dot(pool_ref[...], dpre).astype(BF16)
    for be in range(9):
        p9[32:96, be * 128 : be * 128 + 128] = pooled[be * 64 : be * 64 + 64]
    from_mate.append(send(p9.at[pl.ds(32, 64)], p9m, s_mate.at[5], r_mate.at[5], mate))
    turned[...] = dot_nt(ord2_ref[pl.ds(pl.multiple_of(core * 256, 256), 256), :], taps).astype(BF16)

    def put(chain, j, value):
        value = value.reshape(2, 8, 16, 128)
        for lo in range(2):
            sum_a[chain, lo * 2 + j % 2, j // 2] = value[lo, :CUT]
            sum_b[chain, j // 2, lo * 2 + j % 2] = value[lo, CUT:]

    def put_two(j, value):
        value = value.reshape(2, 8, 16, 128)
        for zz in range(NZ):
            c_sum[zz, j // 2, j % 2] = value[0, zz]
        d_sum[j // 2, j % 2] = value[1]

    from_mate[4].wait_recv()
    shifted(uhm[...], 2, u9m, 256)
    from_mate[3].wait_recv()
    for first in range(0, 9, 2):
        tap = slice(first * 128, min(first * 128 + 256, 1152))
        pair = dot(turned[...], u9[:, tap]) + dot(away_in[...], u9m[:, tap])
        pair = pair.astype(BF16)
        if first == 8:
            put(1, 6, pair)
        else:
            put_two(first, pair[:, 0:128])
            put_two(first + 1, pair[:, 128:256])

    def around(chain, swap):
        copies = []
        src_a, src_b, dst_a, dst_b = (mid_a, mid_b, mid_in_a, mid_in_b) if swap else (sum_a, sum_b, in_a, in_b)
        ssem, rsem = (s_two, r_two) if swap else (s_one, r_one)
        for k in range(1, 4):
            xd, yd = (x + k) % NX, (y + k) % NY
            ia, ib = (yd, xd) if swap else (xd, yd)
            to_a, to_b = (at(yy=yd), at(xx=xd)) if swap else (at(xx=xd), at(yy=yd))
            for src, dst, index, to, n in ((src_a, dst_a, ia, to_a, 2 * k - 2), (src_b, dst_b, ib, to_b, 2 * k - 1)):
                copies.append(send(src.at[chain, index], dst.at[chain, k - 1], ssem.at[chain, n], rsem.at[chain, n], to))
        return copies

    def landed(copies):
        for copy in copies:
            copy.wait_recv()

    def added(own, parts, count):
        total = own.astype(F32)
        for k in range(count):
            total += parts[k].astype(F32)
        return total.astype(BF16)

    def stage_two(chain, copies):
        landed(copies)
        mid_a[chain] = added(sum_a[chain, x], in_a.at[chain], 3)
        mid_b[chain] = added(sum_b[chain, y], in_b.at[chain], 3)
        return around(chain, True)

    def stage_three(chain, copies):
        landed(copies)
        last[chain, 0:CUT] = added(mid_a[chain, y], mid_in_a.at[chain], 3)
        last[chain, CUT:NZ] = added(mid_b[chain, x], mid_in_b.at[chain], 3)
        copies = []
        for k in range(1, NZ):
            zd = (z + k) % NZ
            copies.append(send(
                last.at[chain, zd], last_in.at[chain, k - 1], s_three.at[chain, k - 1], r_three.at[chain, k - 1], at(zz=zd)
            ))
        return copies

    def stage_four(chain, total):
        own[chain] = total
        gath[chain, tm] = total
        copies = []
        for k in range(1, NTM):
            to = at_tm((tm + k) % NTM)
            copies.append(send(own.at[chain], gath.at[chain, tm], s_four.at[chain, k - 1], r_four.at[chain, k - 1], to))
        return copies

    def within(src, dst, ssem, rsem, lo):
        def copy(slot, index, to_hi):
            return pltpu.make_async_remote_copy(
                src_ref=src.at[index], dst_ref=dst.at[slot], send_sem=ssem.at[slot], recv_sem=rsem.at[slot],
                device_id=at(xx=lo * 2 + to_hi), device_id_type=MESH,
            )

        home = (copy(0, 1 - x_hi, 1 - x_hi),)
        abroad = (copy(1, x_hi, x_hi), copy(2, 1 - x_hi, 1 - x_hi))
        return home, abroad

    def each(condition, copies, method):
        @pl.when(condition)
        def _():
            for copy in copies:
                getattr(copy, method)()

    def over_y(src, dst, ssem, rsem):
        copies = []
        for k in range(1, NY):
            yd = (y + k) % NY
            copies.append(send(src.at[yd], dst.at[k - 1], ssem.at[k - 1], rsem.at[k - 1], at(yy=yd)))
        return copies

    c1 = []
    for k in range(1, NZ):
        zd = (z + k) % NZ
        c1.append(send(c_sum.at[zd], c_in.at[k - 1], s_c1.at[k - 1], r_c1.at[k - 1], at(zz=zd)))
    d1 = over_y(d_sum, d_in, s_d1, r_d1)

    from_mate[1].wait_recv()
    from_mate[2].wait_recv()
    feats = []
    mine = pl.ds(pl.multiple_of(core * 128, 128), 128)
    for a in range(3):
        rows = jnp.concatenate([fh[a * 16 : a * 16 + 64, :], fm[a * 16 : a * 16 + 64, :]], axis=0)
        feats.append(dot_nt(ord1_ref[mine, :], rows).astype(BF16))
    from_mate[5].wait_recv()
    units = []
    pools = jnp.concatenate([p9[32:96, :], p9m[...]], axis=0)
    for a in range(3):
        whole = dot(feats[a], pools)
        for be in range(9):
            units.append(whole[:, be * 128 : be * 128 + 128].reshape(16, 8, 128))
            if len(units) == 2:
                tile = (a * 9 + be) // 2
                put(tile // 8, tile % 8, jnp.concatenate(units, axis=1).astype(BF16))
                units = []
    units.append(jnp.zeros((16, 8, 128), F32))
    put(1, 5, jnp.concatenate(units, axis=1).astype(BF16))
    put(1, 7, jnp.zeros((16, 16, 128), BF16))
    f1 = around(0, False)
    l1 = around(1, False)

    result = jnp.zeros((96, 256), F32)
    for a in range(3):
        result += dot_nt(p9[(2 - a) * 16 : (2 - a) * 16 + 96, :], w1_ref[a])
    part[...] = result
    near.append(send(part.at[pl.ds(0, 32)], part_in, s_near.at[2], r_near.at[2], prv))

    landed(d1)
    d_mid[...] = added(d_sum[y], d_in, 3)
    d_home, d_abroad = within(d_mid, d_mid_in, s_d2, r_d2, 1)
    each(x_lo == 1, d_home, "start")
    each(x_lo == 0, d_abroad, "start")
    f2 = stage_two(0, f1)
    l2 = stage_two(1, l1)
    landed(c1)
    c_mid[...] = added(c_sum[z], c_in, 7)
    c2 = over_y(c_mid, c_mid_in, s_c2, r_c2)
    f3 = stage_three(0, f2)

    d3 = []
    for k in range(1, NZ):
        zd = (z + k) % NZ
        d3.append(pltpu.make_async_remote_copy(
            src_ref=d_end.at[zd], dst_ref=d_end_in.at[k - 1], send_sem=s_d3.at[k - 1], recv_sem=r_d3.at[k - 1],
            device_id=at(zz=zd), device_id_type=MESH,
        ))

    @pl.when(x_lo == 1)
    def _():
        for copy in d_home + d_abroad:
            copy.wait_recv()
        d_end[...] = added(d_mid[x_hi], d_mid_in, 3)
        for copy in d3:
            copy.start()

    l3 = stage_three(1, l2)
    landed(c2)
    c_end[...] = added(c_mid[y], c_mid_in, 3)
    c_home, c_abroad = within(c_end, c_end_in, s_c3, r_c3, 0)
    each(x_lo == 0, c_home, "start")
    each(x_lo == 1, c_abroad, "start")
    near[2].wait_recv()
    added_late = jnp.where(tm == NTM - 1, 0.0, part_in[...])
    fg_ref[0:32, :] = part[32:64, :].astype(BF16)
    fg_ref[32:64, :] = (part[64:96, :] + added_late).astype(BF16)
    landed(f3)
    f4 = stage_four(0, added(last[0, z], last_in.at[0], 7))

    @pl.when(x_lo == 0)
    def _():
        for copy in c_home + c_abroad:
            copy.wait_recv()
        final[...] = added(c_end[x_hi], c_end_in, 3)

    @pl.when(x_lo == 1)
    def _():
        for copy in d3:
            copy.wait_recv()
        final[...] = added(d_end[z], d_end_in, 7)

    e4 = stage_four(2, final[...])
    landed(l3)
    l4 = stage_four(1, added(last[1, z], last_in.at[1], 7))

    factor = 1.0 / 256.0
    landed(e4)
    for be in range(8):
        rows = gath[2, be].astype(F32) * factor
        for a in range(3):
            g2_ref[a * 9 + be] = rows[a * 4 : a * 4 + 4]
    landed(f4)
    for tile in range(15):
        if tile == 8:
            landed(l4)
        rows = gath[tile // 8, tile % 8].astype(F32) * factor
        if tile < 14:
            g1_ref[2 * tile] = rows[0:8]
        if tile < 13:
            g1_ref[2 * tile + 1] = rows[8:16]
        if tile == 14:
            for a in range(3):
                g2_ref[a * 9 + 8] = rows[a * 4 : a * 4 + 4]
    each(x_lo == 1, d_home + tuple(d3) + c_abroad, "wait_send")
    each(x_lo == 0, d_abroad + c_home, "wait_send")
    for copy in sent:
        copy.wait_send()


def store(*refs):
    sems = refs[6]
    copies = [pltpu.make_async_copy(refs[i], refs[3 + i], sems.at[i]) for i in range(3)]
    for copy in copies:
        copy.start()
    for copy in copies:
        copy.wait()


def on_device(features, upstream, weight_one, weight_two):
    dma, vmem = pltpu.SemaphoreType.DMA, pltpu.VMEM
    tile = lambda *lead: vmem(lead + (16, 128), BF16)
    pairs = lambda shape: [dma(shape), dma(shape)]
    scratch = [
        vmem((256, 128), BF16), vmem((3, 256, 1152), BF16), vmem((3, 128, 1152), BF16),
        vmem((256, 576), BF16), vmem((576, 256), BF16), vmem((256, 256), BF16), vmem((512, 384), BF16), dma((24,)),
        vmem((96, 256), BF16), vmem((128, 128), BF16), vmem((256, 128), BF16), vmem((128, 128), BF16),
        vmem((96, 256), BF16), vmem((96, 256), BF16),
        vmem((576, 256), BF16), vmem((576, 256), BF16), vmem((384, 1152), BF16), vmem((384, 1152), BF16),
        vmem((512, 128), BF16), vmem((128, 128), F32), vmem((256, 128), F32), vmem((256, 128), F32),
        vmem((128, 1152), BF16), vmem((64, 1152), BF16),
        vmem((256, 384), BF16), vmem((256, 384), BF16), vmem((256, 384), BF16),
        vmem((96, 256), F32), vmem((32, 256), F32),
        tile(2, NX, NY, CUT), tile(2, NY, NX, NZ - CUT), tile(2, 3, NY, CUT), tile(2, 3, NX, NZ - CUT),
        tile(2, NY, CUT), tile(2, NX, NZ - CUT), tile(2, 3, CUT), tile(2, 3, NZ - CUT),
        tile(2, NZ), tile(2, NZ - 1), tile(3), tile(3, NTM),
        tile(), tile(NZ, NY, 2), tile(NZ - 1, NY, 2), tile(NY, 2), tile(3, 2), tile(2), tile(3),
        tile(NY, 2, NZ), tile(3, 2, NZ), tile(2, NZ), tile(3, NZ), tile(NZ), tile(NZ - 1),
    ]
    scratch += pairs((3,)) + pairs((6,)) + pairs((2, 6)) * 2 + pairs((2, 7)) + pairs((3, 7))
    scratch += pairs((7,)) + pairs((3,)) * 4 + pairs((7,))
    spec = pl.BlockSpec(memory_space=pltpu.VMEM)
    shapes = (
        jax.ShapeDtypeStruct((64, 256), BF16),
        jax.ShapeDtypeStruct((27, 8, 128), F32),
        jax.ShapeDtypeStruct((27, 4, 128), F32),
    )
    results = pl.pallas_call(
        kernel,
        out_shape=shapes,
        in_specs=[pl.BlockSpec(memory_space=pltpu.HBM)] * 8,
        out_specs=(spec,) * 3,
        scratch_shapes=scratch,
        compiler_params=pltpu.CompilerParams(
            collective_id=0, has_side_effects=True, vmem_limit_bytes=24 * 1024 * 1024
        ),
    )(
        *(
            pltpu.with_memory_space_constraint(v, pltpu.HBM)
            for v in (
                features.reshape(64, 256),
                upstream.reshape(256, 128),
                weight_one.reshape(3, 9, 256, 128),
                weight_two.reshape(3, 9, 128, 128),
                *tables(),
            )
        )
    )
    fg, one, two = pl.pallas_call(
        store,
        out_shape=shapes,
        in_specs=[spec] * 3,
        out_specs=(pl.BlockSpec(memory_space=pltpu.HBM),) * 3,
        scratch_shapes=[dma((3,))],
    )(*(pltpu.with_memory_space_constraint(v, pltpu.VMEM) for v in results))
    return (
        fg.reshape(features.shape),
        one.reshape(3, 3, 3, 8, 128),
        two.reshape(3, 3, 3, 4, 128),
    )


def solution(mesh):
    wide = P("dp", "tm", None, None, None)
    cut = P(None, None, None, "dp", None)
    return jax.shard_map(
        on_device, mesh=mesh, in_specs=(wide, wide, P(), P()), out_specs=(wide, cut, cut), check_vma=False
    )
```

time: 44.3 us -> 43.4 us (0.980)
  Pallas kernels: 43.6 us -> 42.7 us
    pallas_call x1, Pallas kernels: 42.9 us -> 42 us  [on_device(): pl.pallas_call(kernel, out_shape=shapes, in_specs=[pl.BlockSpec(memory_sp...]
where the time goes in v4:
time: 43.4 us; the launch traced here: 43.3 us
  Pallas kernels  42.7 us (98%)
  between operations  0.64 us (1%)
    pallas_call x1, Pallas kernels, on_device(): pl.pallas_call(kernel, out_shape=shapes, in_specs=[pl.BlockSpec(memory_sp...  42 us

profile of v4, /device:TPU:2, one launch (start us, length us, event | category | flops | bytes accessed | tf_op | source)
XLA Modules:
  0.0 43.3 jit_solution(2540258059962562529)
XLA Ops:
  0.6 42.0 %shard_map.103 = (bf16[64,256]{1,0:T(8,128)(2,1)S(1)}, f32[27,8,128]{2,1,0:T(8,128)S(1)}, f32[27,4,128]{2,1,0:T(4,128)S(1)}) custom-call(bf16[64,256]{1,0:T(8,128)(2,1)} %bitcast.10, bf16[256,128]{1,0:T(8,128)(2,1)} %bitcast.9, bf16[3,9,256,128]{3,2,1,0:T(8,128)(2,1)} %bitcast.7, bf16[3,9,128,128]{3,2,1,0:T(8,128)(2,1)} %bitcast.8, ...), custom_call_target="tpu_custom_call" | custom-call | tf_op jit(solution)/shard_map/pallas_call | solution.py:470
  42.6 0.7 %shard_map.104 = (bf16[64,256]{1,0:T(8,128)(2,1)}, f32[27,8,128]{2,1,0:T(8,128)}, f32[27,4,128]{2,1,0:T(4,128)}) custom-call(bf16[64,256]{1,0:T(8,128)(2,1)S(1)} %get-tuple-element.9.refs_0_, f32[27,8,128]{2,1,0:T(8,128)S(1)} %get-tuple-element.10.refs_1_, f32[27,4,128]{2,1,0:T(4,128)S(1)} %get-tuple-element.11.refs_2_), custom_call_target="tpu_custom_call" | custom-call | tf_op jit(solution)/shard_map/pallas_call | solution.py:491

commit v5 on v4

--- a/solution.py
+++ b/solution.py
@@ -141,14 +141,7 @@
         both = dot(up_ref[0:rows, :], ref[...])
         return both[:, 0:128] + both[:, 128:256]
 
-    ycor[...] = jnp.zeros(ycor.shape, BF16)
-    hid[0:128, :] = jnp.zeros((128, 128), BF16)
-    hid[384:512, :] = jnp.zeros((128, 128), BF16)
-    u9[256:384, :] = jnp.zeros((128, 1152), BF16)
-    p9[0:32, :] = jnp.zeros((32, 1152), BF16)
-    p9[96:128, :] = jnp.zeros((32, 1152), BF16)
     loads[0].wait()
-    shifted(u_ref[...], 4, u9, 0)
     loads[1].wait()
 
     pl.semaphore_wait(barrier, len(peers))
@@ -162,6 +155,13 @@
         send(fh.at[pl.ds(32, 64)], fm.at[pl.ds(32, 64)], s_mate.at[1], r_mate.at[1], mate),
     ]
 
+    ycor[...] = jnp.zeros(ycor.shape, BF16)
+    hid[0:128, :] = jnp.zeros((128, 128), BF16)
+    hid[384:512, :] = jnp.zeros((128, 128), BF16)
+    u9[256:384, :] = jnp.zeros((128, 1152), BF16)
+    p9[0:32, :] = jnp.zeros((32, 1152), BF16)
+    p9[96:128, :] = jnp.zeros((32, 1152), BF16)
+    shifted(u_ref[...], 4, u9, 0)
     for copy in one + loads[2:3]:
         copy.wait()
     fz[0:32, :] = jnp.zeros((32, 256), BF16)
@@ -227,19 +227,6 @@
             c_sum[zz, j // 2, j % 2] = value[0, zz]
         d_sum[j // 2, j % 2] = value[1]
 
-    from_mate[4].wait_recv()
-    shifted(uhm[...], 2, u9m, 256)
-    from_mate[3].wait_recv()
-    for first in range(0, 9, 2):
-        tap = slice(first * 128, min(first * 128 + 256, 1152))
-        pair = dot(turned[...], u9[:, tap]) + dot(away_in[...], u9m[:, tap])
-        pair = pair.astype(BF16)
-        if first == 8:
-            put(1, 6, pair)
-        else:
-            put_two(first, pair[:, 0:128])
-            put_two(first + 1, pair[:, 128:256])
-
     def around(chain, swap):
         copies = []
         src_a, src_b, dst_a, dst_b = (mid_a, mid_b, mid_in_a, mid_in_b) if swap else (sum_a, sum_b, in_a, in_b)
@@ -312,12 +299,6 @@
             yd = (y + k) % NY
             copies.append(send(src.at[yd], dst.at[k - 1], ssem.at[k - 1], rsem.at[k - 1], at(yy=yd)))
         return copies
-
-    c1 = []
-    for k in range(1, NZ):
-        zd = (z + k) % NZ
-        c1.append(send(c_sum.at[zd], c_in.at[k - 1], s_c1.at[k - 1], r_c1.at[k - 1], at(zz=zd)))
-    d1 = over_y(d_sum, d_in, s_d1, r_d1)
 
     from_mate[1].wait_recv()
     from_mate[2].wait_recv()
@@ -337,10 +318,30 @@
                 tile = (a * 9 + be) // 2
                 put(tile // 8, tile % 8, jnp.concatenate(units, axis=1).astype(BF16))
                 units = []
+                if tile == 7:
+                    f1 = around(0, False)
+    from_mate[4].wait_recv()
+    shifted(uhm[...], 2, u9m, 256)
+    from_mate[3].wait_recv()
+    for first in range(0, 9, 2):
+        tap = slice(first * 128, min(first * 128 + 256, 1152))
+        pair = dot(turned[...], u9[:, tap]) + dot(away_in[...], u9m[:, tap])
+        pair = pair.astype(BF16)
+        if first == 8:
+            put(1, 6, pair)
+        else:
+            put_two(first, pair[:, 0:128])
+            put_two(first + 1, pair[:, 128:256])
+
+    d1 = over_y(d_sum, d_in, s_d1, r_d1)
+    c1 = []
+    for k in range(1, NZ):
+        zd = (z + k) % NZ
+        c1.append(send(c_sum.at[zd], c_in.at[k - 1], s_c1.at[k - 1], r_c1.at[k - 1], at(zz=zd)))
+
     units.append(jnp.zeros((16, 8, 128), F32))
     put(1, 5, jnp.concatenate(units, axis=1).astype(BF16))
     put(1, 7, jnp.zeros((16, 16, 128), BF16))
-    f1 = around(0, False)
     l1 = around(1, False)
 
     result = jnp.zeros((96, 256), F32)
@@ -355,10 +356,10 @@
     each(x_lo == 1, d_home, "start")
     each(x_lo == 0, d_abroad, "start")
     f2 = stage_two(0, f1)
-    l2 = stage_two(1, l1)
     landed(c1)
     c_mid[...] = added(c_sum[z], c_in, 7)
     c2 = over_y(c_mid, c_mid_in, s_c2, r_c2)
+    l2 = stage_two(1, l1)
     f3 = stage_three(0, f2)
 
     d3 = []

time: 43.4 us -> 42.7 us (0.984)
  Pallas kernels: 42.7 us -> 41.6 us
    pallas_call x1, Pallas kernels: 42 us -> 40.9 us  [on_device(): pl.pallas_call(kernel, out_shape=shapes, in_specs=[pl.BlockSpec(memory_sp...]
where the time goes in v5:
time: 42.7 us; the launch traced here: 42.2 us
  Pallas kernels  41.6 us (97%)
  between operations  0.64 us (1%)
    pallas_call x1, Pallas kernels, on_device(): pl.pallas_call(kernel, out_shape=shapes, in_specs=[pl.BlockSpec(memory_sp...  40.9 us

profile of v5, /device:TPU:2, one launch (start us, length us, event | category | flops | bytes accessed | tf_op | source)
XLA Modules:
  0.0 42.2 jit_solution(11933086514067931438)
XLA Ops:
  0.6 40.9 %shard_map.103 = (bf16[64,256]{1,0:T(8,128)(2,1)S(1)}, f32[27,8,128]{2,1,0:T(8,128)S(1)}, f32[27,4,128]{2,1,0:T(4,128)S(1)}) custom-call(bf16[64,256]{1,0:T(8,128)(2,1)} %bitcast.10, bf16[256,128]{1,0:T(8,128)(2,1)} %bitcast.9, bf16[3,9,256,128]{3,2,1,0:T(8,128)(2,1)} %bitcast.7, bf16[3,9,128,128]{3,2,1,0:T(8,128)(2,1)} %bitcast.8, ...), custom_call_target="tpu_custom_call" | custom-call | tf_op jit(solution)/shard_map/pallas_call | solution.py:471
  41.5 0.7 %shard_map.104 = (bf16[64,256]{1,0:T(8,128)(2,1)}, f32[27,8,128]{2,1,0:T(8,128)}, f32[27,4,128]{2,1,0:T(4,128)}) custom-call(bf16[64,256]{1,0:T(8,128)(2,1)S(1)} %get-tuple-element.9.refs_0_, f32[27,8,128]{2,1,0:T(8,128)S(1)} %get-tuple-element.10.refs_1_, f32[27,4,128]{2,1,0:T(4,128)S(1)} %get-tuple-element.11.refs_2_), custom_call_target="tpu_custom_call" | custom-call | tf_op jit(solution)/shard_map/pallas_call | solution.py:492

commit v6 on v5

--- a/solution.py
+++ b/solution.py
@@ -10,6 +10,7 @@
 F32, BF16 = jnp.float32, jnp.bfloat16
 
 NZ, NX, NY, NTM = 8, 4, 4, 8
+FAR_Z, FAR_TM = (4, 3, 5, 2, 6, 1, 7), (5, 3, 4, 1, 7, 2, 6)
 CUT = 5
 
 
@@ -231,12 +232,21 @@
         copies = []
         src_a, src_b, dst_a, dst_b = (mid_a, mid_b, mid_in_a, mid_in_b) if swap else (sum_a, sum_b, in_a, in_b)
         ssem, rsem = (s_two, r_two) if swap else (s_one, r_one)
-        for k in range(1, 4):
+        for k in (1, 2, 3, 0) if swap else (1, 2, 3):
             xd, yd = (x + k) % NX, (y + k) % NY
             ia, ib = (yd, xd) if swap else (xd, yd)
             to_a, to_b = (at(yy=yd), at(xx=xd)) if swap else (at(xx=xd), at(yy=yd))
             for src, dst, index, to, n in ((src_a, dst_a, ia, to_a, 2 * k - 2), (src_b, dst_b, ib, to_b, 2 * k - 1)):
-                copies.append(send(src.at[chain, index], dst.at[chain, k - 1], ssem.at[chain, n], rsem.at[chain, n], to))
+                if swap:
+                    held, parts, place = (sum_a, in_a, x) if src is src_a else (sum_b, in_b, y)
+                    total = held[chain, place, index].astype(F32)
+                    for m in range(3):
+                        total += parts[chain, m, index].astype(F32)
+                    src[chain, index] = total.astype(BF16)
+                if k:
+                    copies.append(
+                        send(src.at[chain, index], dst.at[chain, k - 1], ssem.at[chain, n], rsem.at[chain, n], to)
+                    )
         return copies
 
     def landed(copies):
@@ -251,8 +261,6 @@
 
     def stage_two(chain, copies):
         landed(copies)
-        mid_a[chain] = added(sum_a[chain, x], in_a.at[chain], 3)
-        mid_b[chain] = added(sum_b[chain, y], in_b.at[chain], 3)
         return around(chain, True)
 
     def stage_three(chain, copies):
@@ -260,7 +268,7 @@
         last[chain, 0:CUT] = added(mid_a[chain, y], mid_in_a.at[chain], 3)
         last[chain, CUT:NZ] = added(mid_b[chain, x], mid_in_b.at[chain], 3)
         copies = []
-        for k in range(1, NZ):
+        for k in FAR_Z:
             zd = (z + k) % NZ
             copies.append(send(
                 last.at[chain, zd], last_in.at[chain, k - 1], s_three.at[chain, k - 1], r_three.at[chain, k - 1], at(zz=zd)
@@ -271,7 +279,7 @@
         own[chain] = total
         gath[chain, tm] = total
         copies = []
-        for k in range(1, NTM):
+        for k in FAR_TM:
             to = at_tm((tm + k) % NTM)
             copies.append(send(own.at[chain], gath.at[chain, tm], s_four.at[chain, k - 1], r_four.at[chain, k - 1], to))
         return copies
@@ -335,7 +343,7 @@
 
     d1 = over_y(d_sum, d_in, s_d1, r_d1)
     c1 = []
-    for k in range(1, NZ):
+    for k in FAR_Z:
         zd = (z + k) % NZ
         c1.append(send(c_sum.at[zd], c_in.at[k - 1], s_c1.at[k - 1], r_c1.at[k - 1], at(zz=zd)))
 
@@ -356,14 +364,14 @@
     each(x_lo == 1, d_home, "start")
     each(x_lo == 0, d_abroad, "start")
     f2 = stage_two(0, f1)
+    l2 = stage_two(1, l1)
     landed(c1)
     c_mid[...] = added(c_sum[z], c_in, 7)
     c2 = over_y(c_mid, c_mid_in, s_c2, r_c2)
-    l2 = stage_two(1, l1)
     f3 = stage_three(0, f2)
 
     d3 = []
-    for k in range(1, NZ):
+    for k in FAR_Z:
         zd = (z + k) % NZ
         d3.append(pltpu.make_async_remote_copy(
             src_ref=d_end.at[zd], dst_ref=d_end_in.at[k - 1], send_sem=s_d3.at[k - 1], recv_sem=r_d3.at[k - 1],

time: 42.7 us -> 42.4 us (level)
  no operation moved by 1% of the time
where the time goes in v6:
time: 42.4 us; the launch traced here: 42.3 us
  Pallas kernels  41.7 us (98%)
  between operations  0.64 us (2%)
    pallas_call x1, Pallas kernels, on_device(): pl.pallas_call(kernel, out_shape=shapes, in_specs=[pl.BlockSpec(memory_sp...  41 us

profile of v6, /device:TPU:2, one launch (start us, length us, event | category | flops | bytes accessed | tf_op | source)
XLA Modules:
  0.0 42.3 jit_solution(3283480887061712141)
XLA Ops:
  0.6 41.0 %shard_map.103 = (bf16[64,256]{1,0:T(8,128)(2,1)S(1)}, f32[27,8,128]{2,1,0:T(8,128)S(1)}, f32[27,4,128]{2,1,0:T(4,128)S(1)}) custom-call(bf16[64,256]{1,0:T(8,128)(2,1)} %bitcast.10, bf16[256,128]{1,0:T(8,128)(2,1)} %bitcast.9, bf16[3,9,256,128]{3,2,1,0:T(8,128)(2,1)} %bitcast.7, bf16[3,9,128,128]{3,2,1,0:T(8,128)(2,1)} %bitcast.8, ...), custom_call_target="tpu_custom_call" | custom-call | tf_op jit(solution)/shard_map/pallas_call | solution.py:479
  41.6 0.7 %shard_map.104 = (bf16[64,256]{1,0:T(8,128)(2,1)}, f32[27,8,128]{2,1,0:T(8,128)}, f32[27,4,128]{2,1,0:T(4,128)}) custom-call(bf16[64,256]{1,0:T(8,128)(2,1)S(1)} %get-tuple-element.9.refs_0_, f32[27,8,128]{2,1,0:T(8,128)S(1)} %get-tuple-element.10.refs_1_, f32[27,4,128]{2,1,0:T(4,128)S(1)} %get-tuple-element.11.refs_2_), custom_call_target="tpu_custom_call" | custom-call | tf_op jit(solution)/shard_map/pallas_call | solution.py:500

commit v7 on v6

--- a/solution.py
+++ b/solution.py
@@ -232,7 +232,7 @@
         copies = []
         src_a, src_b, dst_a, dst_b = (mid_a, mid_b, mid_in_a, mid_in_b) if swap else (sum_a, sum_b, in_a, in_b)
         ssem, rsem = (s_two, r_two) if swap else (s_one, r_one)
-        for k in (1, 2, 3, 0) if swap else (1, 2, 3):
+        for k in (2, 1, 3, 0) if swap else (2, 1, 3):
             xd, yd = (x + k) % NX, (y + k) % NY
             ia, ib = (yd, xd) if swap else (xd, yd)
             to_a, to_b = (at(yy=yd), at(xx=xd)) if swap else (at(xx=xd), at(yy=yd))

time: 42.4 us -> 42.3 us (level)
  no operation moved by 1% of the time
where the time goes in v7:
time: 42.3 us; the launch traced here: 42.1 us
  Pallas kernels  41.4 us (98%)
  between operations  0.64 us (2%)
    pallas_call x1, Pallas kernels, on_device(): pl.pallas_call(kernel, out_shape=shapes, in_specs=[pl.BlockSpec(memory_sp...  40.7 us

profile of v7, /device:TPU:2, one launch (start us, length us, event | category | flops | bytes accessed | tf_op | source)
XLA Modules:
  0.0 42.1 jit_solution(17734394713251746)
XLA Ops:
  0.6 40.7 %shard_map.103 = (bf16[64,256]{1,0:T(8,128)(2,1)S(1)}, f32[27,8,128]{2,1,0:T(8,128)S(1)}, f32[27,4,128]{2,1,0:T(4,128)S(1)}) custom-call(bf16[64,256]{1,0:T(8,128)(2,1)} %bitcast.10, bf16[256,128]{1,0:T(8,128)(2,1)} %bitcast.9, bf16[3,9,256,128]{3,2,1,0:T(8,128)(2,1)} %bitcast.7, bf16[3,9,128,128]{3,2,1,0:T(8,128)(2,1)} %bitcast.8, ...), custom_call_target="tpu_custom_call" | custom-call | tf_op jit(solution)/shard_map/pallas_call | solution.py:479
  41.4 0.7 %shard_map.104 = (bf16[64,256]{1,0:T(8,128)(2,1)}, f32[27,8,128]{2,1,0:T(8,128)}, f32[27,4,128]{2,1,0:T(4,128)}) custom-call(bf16[64,256]{1,0:T(8,128)(2,1)S(1)} %get-tuple-element.9.refs_0_, f32[27,8,128]{2,1,0:T(8,128)S(1)} %get-tuple-element.10.refs_1_, f32[27,4,128]{2,1,0:T(4,128)S(1)} %get-tuple-element.11.refs_2_), custom_call_target="tpu_custom_call" | custom-call | tf_op jit(solution)/shard_map/pallas_call | solution.py:500
